TPU v7x, 128 devices: a whole 4x4x4 slice. The times are simulated.
128 devices in a mesh: ta: 8 (over y, core), gx: 16 (over z, x).
Axes of the slice: x: 4, y: 4, z: 4, core: 2. Of those that a mesh axis runs over, the one named last changes fastest.
Arguments:
- gauge_links: float32 [4, 2, 3, 3, 16, 64, 256], P(None, None, None, None, 'ta', 'gx'), may hold values from -1 to 1, as said below
Outputs:
- rotated: float32 [4, 2, 3, 3, 16, 64, 256], P(None, None, None, None, 'ta', 'gx')
Inputs may be any that keep to these rules, and one draw needn't show every extreme that they name: `gauge_links`: every link is a special unitary 3 x 3 matrix.
All inputs are finite; a program needn't handle non-finite values.
Results may differ from a plain program's by a relative error of at most 0.0003.
Values sent between devices are 32-bit elements; how exact they have to be, the bound alone decides.
A program may use at most 64 MiB of HBM per device.

v0:
```python
import jax
import jax.numpy as jnp
from jax import lax
from jax.sharding import PartitionSpec as P

NZ = 16
NEWTON = 5


ape_weight = 0.4


def padded_2(array, sides, width):
    for axis, dim in sides:
        size, length = (lax.axis_size(axis), array.shape[dim])
        up = [(i, (i + 1) % size) for i in range(size)]
        down = [(j, i) for i, j in up]
        last = lax.slice_in_dim(array, length - width, length, axis=dim)
        initial = lax.slice_in_dim(array, 0, width, axis=dim)
        before = lax.ppermute(last, axis, up)
        after = lax.ppermute(initial, axis, down)
        array = jnp.concatenate([before, array, after], axis=dim)
    return array


def entering(value, axis, join, neutral):
    count, mine = (lax.axis_size(axis), lax.axis_index(axis))
    pieces = lax.all_gather(value, axis)
    total = jnp.full_like(value, 0) + jnp.asarray(neutral, value.dtype)

    def hop(position, total):
        longer = join(total, pieces[position])
        return jnp.where(position < mine, longer, total)

    return lax.fori_loop(0, count - 1, hop, total)


def shifted_2(value, axis, steps):
    count = lax.axis_size(axis)
    pairs = [(source, (source + steps) % count) for source in range(count)]
    return lax.ppermute(value, axis, pairs)


def matmul_pair(left_mat, right_mat):
    real_part = (
        left_mat[0][:, 0, None] * right_mat[0][None, 0]
        - left_mat[1][:, 0, None] * right_mat[1][None, 0]
    )
    imag_part = (
        left_mat[0][:, 0, None] * right_mat[1][None, 0]
        + left_mat[1][:, 0, None] * right_mat[0][None, 0]
    )
    for column in (1, 2):
        real_part = (
            real_part
            + left_mat[0][:, column, None] * right_mat[0][None, column]
            - left_mat[1][:, column, None] * right_mat[1][None, column]
        )
        imag_part = (
            imag_part
            + left_mat[0][:, column, None] * right_mat[1][None, column]
            + left_mat[1][:, column, None] * right_mat[0][None, column]
        )
    return jnp.stack([real_part, imag_part])


def dagger_of(matrix):
    return jnp.stack([jnp.swapaxes(matrix[0], 0, 1), -jnp.swapaxes(matrix[1], 0, 1)])


def identity_like(template):
    tail = template.shape[3:]
    real_part = jnp.broadcast_to(
        jnp.eye(3, dtype=jnp.float32).reshape((3, 3) + (1,) * len(tail)), (3, 3) + tail
    )
    return jnp.stack([real_part, jnp.zeros_like(real_part)])


def yz_roll(source, shift_y, shift_z):
    moved = source
    if shift_y != 0:
        moved = jnp.roll(moved, -NZ * shift_y, axis=-1)
    if shift_z != 0:
        z_place = lax.broadcasted_iota(jnp.int32, (moved.shape[-1],), 0) % NZ
        target = z_place + shift_z
        inside = (target >= 0) & (target < NZ)
        plain = jnp.roll(moved, -shift_z, axis=-1)
        if shift_z > 0:
            wrapped = jnp.roll(moved, NZ - shift_z, axis=-1)
        else:
            wrapped = jnp.roll(moved, -(NZ + shift_z), axis=-1)
        moved = jnp.where(inside, plain, wrapped)
    return moved


def shifted(source, offset):
    time_len = source.shape[-3]
    space_len = source.shape[-2]
    moved_part = source[
        ..., 1 + offset[0] : time_len - 1 + offset[0], 1 + offset[1] : space_len - 1 + offset[1], :
    ]
    return yz_roll(moved_part, offset[2], offset[3])


def unit_offset(direction):
    return tuple((1 if axis_pos == direction else 0 for axis_pos in range(4)))


def unitarise(blended):
    three_eye = 3.0 * identity_like(blended)
    frobenius = jnp.sqrt(jnp.sum(blended * blended, axis=(0, 1, 2)))
    current = blended / jnp.maximum(frobenius, 1.0)
    for repeat in range(NEWTON):
        current = 0.5 * matmul_pair(current, three_eye - matmul_pair(dagger_of(current), current))
    return current


def smear(gauge_links, mover):
    result = []
    anchor = (0, 0, 0, 0)
    for direction in range(4):
        step_dir = unit_offset(direction)
        staple_sum = None
        for other in range(4):
            if other == direction:
                continue
            step_other = unit_offset(other)
            back_other = tuple((-value for value in step_other))
            diagonal_step = tuple((first - second for first, second in zip(step_dir, step_other)))
            upper_path = matmul_pair(
                matmul_pair(
                    mover(gauge_links[other], anchor), mover(gauge_links[direction], step_other)
                ),
                dagger_of(mover(gauge_links[other], step_dir)),
            )
            lower_path = matmul_pair(
                matmul_pair(
                    dagger_of(mover(gauge_links[other], back_other)),
                    mover(gauge_links[direction], back_other),
                ),
                mover(gauge_links[other], diagonal_step),
            )
            if staple_sum is None:
                staple_sum = upper_path + lower_path
            else:
                staple_sum = staple_sum + upper_path + lower_path
        blended = (1.0 - ape_weight) * mover(
            gauge_links[direction], anchor
        ) + ape_weight / 6.0 * staple_sum
        result.append(unitarise(blended))
    return jnp.stack(result)


def body(gauge_links):
    current = gauge_links
    for repeat in range(2):
        padded = padded_2(current, (("ta", 4), ("gx", 5)), 1)
        current = smear(padded, shifted)
    temporal = current[0]
    running = identity_like(temporal[:, :, :, 0])
    before_list = []
    after_list = []
    for slice_pos in range(temporal.shape[3]):
        before_list.append(running)
        running = matmul_pair(running, temporal[:, :, :, slice_pos])
        after_list.append(running)
    carried = entering(running, "ta", matmul_pair, identity_like(running))
    carried_wide = carried[:, :, :, None]
    rotation = matmul_pair(carried_wide, jnp.stack(before_list, 3))
    after_rot = matmul_pair(carried_wide, jnp.stack(after_list, 3))
    first_slice = rotation[:, :, :, :, 0:1, :]
    from_next = shifted_2(first_slice, "gx", -1)
    x_next = jnp.concatenate([rotation[:, :, :, :, 1:, :], from_next], axis=4)
    neighbours = [after_rot, x_next, yz_roll(rotation, 1, 0), yz_roll(rotation, 0, 1)]
    result = []
    for direction in range(4):
        result.append(
            matmul_pair(matmul_pair(rotation, current[direction]), dagger_of(neighbours[direction]))
        )
    return jnp.stack(result)


def solution(mesh):
    in_specs = (P(None, None, None, None, "ta", "gx", None),)
    out_specs = P(None, None, None, None, "ta", "gx", None)
    return jax.shard_map(body, mesh=mesh, in_specs=in_specs, out_specs=out_specs, check_vma=False)
```

profile of v0, /device:TPU:1, one launch (start us, length us, event | category | flops | bytes accessed | tf_op | source)
XLA Modules:
  0.0 141.3 jit_solution(14746012112755912868)
XLA Ops:
  0.0 1.1 fusion.385
  1.1 1.4 %collective-permute-start.1 = (f32[4,2,3,3,1,4,256]{6,5,4,3,2,1,0:T(4,128)S(1)}, f32[4,2,3,3,1,4,256]{6,5,4,3,2,1,0:T(4,128)S(1)}, u32[]{:S(2)}, u32[]{:S(2)}) collective-permute-start(f32[4,2,3,3,1,4,256]{6,5,4,3,2,1,0:T(4,128)S(1)} %get-tuple-element.143), channel_id=1, source_target_pairs={{16,0},{32,16},{48,32},{64,48},{80,64},{96,80},{112,96},{0,112},{1... | collective-permute-start | bytes 884744 | tf_op jit(solution)/shard_map/ppermute | solution.py:21
  2.5 1.3 collective-permute-start
  3.8 1.4 copy.718
  5.2 3.0 %collective-permute-done.1 = f32[4,2,3,3,1,4,256]{6,5,4,3,2,1,0:T(4,128)S(1)} collective-permute-done((f32[4,2,3,3,1,4,256]{6,5,4,3,2,1,0:T(4,128)S(1)}, f32[4,2,3,3,1,4,256]{6,5,4,3,2,1,0:T(4,128)S(1)}, u32[]{:S(2)}, u32[]{:S(2)}) %collective-permute-start.1) | collective-permute-done | bytes 294944 | tf_op jit(solution)/shard_map/ppermute | solution.py:21
  8.9 0.4 pad_maximum_fusion.12
  9.3 6.0 %collective-permute-start.3 = (f32[4,2,3,3,4,1,256]{6,4,5,3,2,1,0:T(4,128)S(1)}, f32[4,2,3,3,4,1,256]{6,4,5,3,2,1,0:T(4,128)S(1)}, u32[]{:S(2)}, u32[]{:S(2)}) collective-permute-start(f32[4,2,3,3,4,1,256]{6,4,5,3,2,1,0:T(4,128)S(1)} %get-tuple-element.139), channel_id=1, source_target_pairs={{1,0},{2,1},{3,2},{4,3},{5,4},{6,5},{7,6},{8,7},{9,8},{10,9},{11,1... | collective-permute-start | bytes 884744 | tf_op jit(solution)/shard_map/ppermute | solution.py:21
  15.6 3.4 %collective-permute-done.3 = f32[4,2,3,3,4,1,256]{6,4,5,3,2,1,0:T(4,128)S(1)} collective-permute-done((f32[4,2,3,3,4,1,256]{6,4,5,3,2,1,0:T(4,128)S(1)}, f32[4,2,3,3,4,1,256]{6,4,5,3,2,1,0:T(4,128)S(1)}, u32[]{:S(2)}, u32[]{:S(2)}) %collective-permute-start.3) | collective-permute-done | bytes 294944 | tf_op jit(solution)/shard_map/ppermute | solution.py:21
  19.0 5.4 %collective-permute-done.2 = f32[4,2,3,3,4,1,256]{6,4,5,3,2,1,0:T(4,128)S(1)} collective-permute-done((f32[4,2,3,3,4,1,256]{6,4,5,3,2,1,0:T(4,128)S(1)}, f32[4,2,3,3,4,1,256]{6,4,5,3,2,1,0:T(4,128)S(1)}, u32[]{:S(2)}, u32[]{:S(2)}) %collective-permute-start.2) | collective-permute-done | bytes 294944 | tf_op jit(solution)/shard_map/ppermute | solution.py:20
  24.3 0.9 pad_maximum_fusion
  25.6 0.5 fusion.417
  26.1 0.4 fusion.416
  26.9 0.7 fusion.414
  28.0 0.5 fusion.424
  28.5 0.6 fusion.427
  29.7 0.6 fusion.423
  31.5 0.5 fusion.411
  32.9 1.1 maximum_select_fusion.3
  34.1 0.8 maximum_select_fusion.2
  35.2 1.1 maximum_select_fusion.1
  36.5 0.4 fusion.60
  39.1 0.4 multiply_reduce_fusion.7
  43.3 0.4 multiply_reduce_fusion.6
  45.6 0.4 multiply_reduce_fusion.5
  47.0 0.7 maximum_select_fusion.12
  49.1 0.5 multiply_reduce_fusion.4
  50.0 0.5 multiply_subtract_fusion.129
  59.0 0.5 fusion.384
  59.4 5.3 %collective-permute-start.5 = (f32[4,2,3,3,1,4,256]{6,4,5,3,2,1,0:T(1,128)S(1)}, f32[4,2,3,3,1,4,256]{6,4,5,3,2,1,0:T(1,128)S(1)}, u32[]{:S(2)}, u32[]{:S(2)}) collective-permute-start(f32[4,2,3,3,1,4,256]{6,4,5,3,2,1,0:T(1,128)S(1)} %get-tuple-element.141), channel_id=1, source_target_pairs={{16,0},{32,16},{48,32},{64,48},{80,64},{96,80},{112,96},{0,112},{1... | collective-permute-start | bytes 884744 | tf_op jit(solution)/shard_map/ppermute | solution.py:21
  64.8 4.3 %collective-permute-done.5 = f32[4,2,3,3,1,4,256]{6,4,5,3,2,1,0:T(1,128)S(1)} collective-permute-done((f32[4,2,3,3,1,4,256]{6,4,5,3,2,1,0:T(1,128)S(1)}, f32[4,2,3,3,1,4,256]{6,4,5,3,2,1,0:T(1,128)S(1)}, u32[]{:S(2)}, u32[]{:S(2)}) %collective-permute-start.5) | collective-permute-done | bytes 294944 | tf_op jit(solution)/shard_map/ppermute | solution.py:21
  69.1 0.4 pad_maximum_fusion.9
  69.6 1.5 %collective-permute-start.6 = (f32[4,2,3,3,4,1,256]{6,4,5,3,2,1,0:T(4,128)S(1)}, f32[4,2,3,3,4,1,256]{6,4,5,3,2,1,0:T(4,128)S(1)}, u32[]{:S(2)}, u32[]{:S(2)}) collective-permute-start(f32[4,2,3,3,4,1,256]{6,4,5,3,2,1,0:T(4,128)S(1)} %get-tuple-element.136), channel_id=1, source_target_pairs={{0,1},{1,2},{2,3},{3,4},{4,5},{5,6},{6,7},{7,8},{8,9},{9,10},{10,1... | collective-permute-start | bytes 884744 | tf_op jit(solution)/shard_map/ppermute | solution.py:20
  71.1 4.0 %collective-permute-done.7 = f32[4,2,3,3,4,1,256]{6,4,5,3,2,1,0:T(4,128)S(1)} collective-permute-done((f32[4,2,3,3,4,1,256]{6,4,5,3,2,1,0:T(4,128)S(1)}, f32[4,2,3,3,4,1,256]{6,4,5,3,2,1,0:T(4,128)S(1)}, u32[]{:S(2)}, u32[]{:S(2)}) %collective-permute-start.7) | collective-permute-done | bytes 294944 | tf_op jit(solution)/shard_map/ppermute | solution.py:21
  75.1 3.4 %collective-permute-done.6 = f32[4,2,3,3,4,1,256]{6,4,5,3,2,1,0:T(4,128)S(1)} collective-permute-done((f32[4,2,3,3,4,1,256]{6,4,5,3,2,1,0:T(4,128)S(1)}, f32[4,2,3,3,4,1,256]{6,4,5,3,2,1,0:T(4,128)S(1)}, u32[]{:S(2)}, u32[]{:S(2)}) %collective-permute-start.6) | collective-permute-done | bytes 294944 | tf_op jit(solution)/shard_map/ppermute | solution.py:20
  78.5 1.2 pad_maximum_fusion.1
  80.8 0.5 fusion.394
  87.4 0.8 maximum_select_fusion.19
  88.2 1.1 maximum_select_fusion.18
  89.6 1.1 maximum_select_fusion.23
  93.4 0.4 multiply_reduce_fusion.2
  98.7 0.4 multiply_reduce_fusion.3
  101.2 0.5 multiply_reduce_fusion.1
  102.3 0.7 maximum_select_fusion.24
  104.0 0.5 multiply_reduce_fusion
  112.9 19.5 %all-gather = f32[16,3,3,4,256]{4,3,2,1,0:T(4,128)S(1)} all-gather(f32[2,3,3,4,256]{4,3,2,1,0:T(4,128)S(1)} %get-tuple-element.1875), channel_id=2, replica_groups=mesh['ta'=8,'gx'=16] {'ta'}, dimensions={0}, use_global_device_ids=true | all-gather | bytes 663552 | tf_op jit(solution)/shard_map/all_gather | solution.py:28
  132.4 1.5 %while.13 = (s32[]{:T(128)}, f32[2,3,3,4,256]{4,3,2,1,0:T(4,128)S(1)}, s32[]{:T(128)}, f32[8,2,3,3,4,256]{5,4,3,2,1,0:T(4,128)S(1)}, s32[]{:T(128)}, /*index=5*/s32[]{:T(128)}, s32[]{}, s32[]{}) while((s32[]{:T(128)}, f32[2,3,3,4,256]{4,3,2,1,0:T(4,128)S(1)}, s32[]{:T(128)}, f32[8,2,3,3,4,256]{5,4,3,2,1,0:T(4,128)S(1)}, s32[]{:T(128)}, ...), condition=%wide.region_6.7_spmd, body=%wide.region_5.6_spmd.sunk | while | flops 239621 | bytes 884875 | solution.py:35
  138.0 1.6 %collective-permute-done.8 = f32[2,3,3,2,1,256]{5,3,4,2,1,0:T(2,128)S(1)} collective-permute-done((f32[2,3,3,2,1,256]{5,3,4,2,1,0:T(2,128)S(1)}, f32[2,3,3,2,1,256]{5,3,4,2,1,0:T(2,128)S(1)}, u32[]{:S(2)}, u32[]{:S(2)}) %collective-permute-start.8) | collective-permute-done | bytes 36896 | tf_op jit(solution)/shard_map/ppermute | solution.py:41
  139.9 0.9 pad_maximum_fusion.3
  (1028 shorter events, 50.6 us)
Async XLA Ops:
  1.1 7.1 %collective-permute-start.1 = (f32[4,2,3,3,1,4,256]{6,5,4,3,2,1,0:T(4,128)S(1)}, f32[4,2,3,3,1,4,256]{6,5,4,3,2,1,0:T(4,128)S(1)}, u32[]{:S(2)}, u32[]{:S(2)}) collective-permute-start(f32[4,2,3,3,1,4,256]{6,5,4,3,2,1,0:T(4,128)S(1)} %get-tuple-element.143), channel_id=1, source_target_pairs={{16,0},{32,16},{48,32},{64,48},{80,64},{96,80},{112,96},{0,112},{1... | collective-permute-start | bytes 884744 | tf_op jit(solution)/shard_map/ppermute | solution.py:21
  2.5 6.0 %collective-permute-start = (f32[4,2,3,3,1,4,256]{6,5,4,3,2,1,0:T(4,128)S(1)}, f32[4,2,3,3,1,4,256]{6,5,4,3,2,1,0:T(4,128)S(1)}, u32[]{:S(2)}, u32[]{:S(2)}) collective-permute-start(f32[4,2,3,3,1,4,256]{6,5,4,3,2,1,0:T(4,128)S(1)} %get-tuple-element.142), channel_id=1, source_target_pairs={{0,16},{16,32},{32,48},{48,64},{64,80},{80,96},{96,112},{112,0},{1... | collective-permute-start | bytes 884744 | tf_op jit(solution)/shard_map/ppermute | solution.py:20
  9.3 9.7 %collective-permute-start.3 = (f32[4,2,3,3,4,1,256]{6,4,5,3,2,1,0:T(4,128)S(1)}, f32[4,2,3,3,4,1,256]{6,4,5,3,2,1,0:T(4,128)S(1)}, u32[]{:S(2)}, u32[]{:S(2)}) collective-permute-start(f32[4,2,3,3,4,1,256]{6,4,5,3,2,1,0:T(4,128)S(1)} %get-tuple-element.139), channel_id=1, source_target_pairs={{1,0},{2,1},{3,2},{4,3},{5,4},{6,5},{7,6},{8,7},{9,8},{10,9},{11,1... | collective-permute-start | bytes 884744 | tf_op jit(solution)/shard_map/ppermute | solution.py:21
  15.3 9.0 %collective-permute-start.2 = (f32[4,2,3,3,4,1,256]{6,4,5,3,2,1,0:T(4,128)S(1)}, f32[4,2,3,3,4,1,256]{6,4,5,3,2,1,0:T(4,128)S(1)}, u32[]{:S(2)}, u32[]{:S(2)}) collective-permute-start(f32[4,2,3,3,4,1,256]{6,4,5,3,2,1,0:T(4,128)S(1)} %get-tuple-element.138), channel_id=1, source_target_pairs={{0,1},{1,2},{2,3},{3,4},{4,5},{5,6},{6,7},{7,8},{8,9},{9,10},{10,1... | collective-permute-start | bytes 884744 | tf_op jit(solution)/shard_map/ppermute | solution.py:20
  59.4 9.6 %collective-permute-start.5 = (f32[4,2,3,3,1,4,256]{6,4,5,3,2,1,0:T(1,128)S(1)}, f32[4,2,3,3,1,4,256]{6,4,5,3,2,1,0:T(1,128)S(1)}, u32[]{:S(2)}, u32[]{:S(2)}) collective-permute-start(f32[4,2,3,3,1,4,256]{6,4,5,3,2,1,0:T(1,128)S(1)} %get-tuple-element.141), channel_id=1, source_target_pairs={{16,0},{32,16},{48,32},{64,48},{80,64},{96,80},{112,96},{0,112},{1... | collective-permute-start | bytes 884744 | tf_op jit(solution)/shard_map/ppermute | solution.py:21
  64.8 4.3 %collective-permute-start.4 = (f32[4,2,3,3,1,4,256]{6,4,5,3,2,1,0:T(1,128)S(1)}, f32[4,2,3,3,1,4,256]{6,4,5,3,2,1,0:T(1,128)S(1)}, u32[]{:S(2)}, u32[]{:S(2)}) collective-permute-start(f32[4,2,3,3,1,4,256]{6,4,5,3,2,1,0:T(1,128)S(1)} %get-tuple-element.140), channel_id=1, source_target_pairs={{0,16},{16,32},{32,48},{48,64},{64,80},{80,96},{96,112},{112,0},{1... | collective-permute-start | bytes 884744 | tf_op jit(solution)/shard_map/ppermute | solution.py:20
  69.5 5.6 %collective-permute-start.7 = (f32[4,2,3,3,4,1,256]{6,4,5,3,2,1,0:T(4,128)S(1)}, f32[4,2,3,3,4,1,256]{6,4,5,3,2,1,0:T(4,128)S(1)}, u32[]{:S(2)}, u32[]{:S(2)}) collective-permute-start(f32[4,2,3,3,4,1,256]{6,4,5,3,2,1,0:T(4,128)S(1)} %get-tuple-element.137), channel_id=1, source_target_pairs={{1,0},{2,1},{3,2},{4,3},{5,4},{6,5},{7,6},{8,7},{9,8},{10,9},{11,1... | collective-permute-start | bytes 884744 | tf_op jit(solution)/shard_map/ppermute | solution.py:21
  69.6 9.0 %collective-permute-start.6 = (f32[4,2,3,3,4,1,256]{6,4,5,3,2,1,0:T(4,128)S(1)}, f32[4,2,3,3,4,1,256]{6,4,5,3,2,1,0:T(4,128)S(1)}, u32[]{:S(2)}, u32[]{:S(2)}) collective-permute-start(f32[4,2,3,3,4,1,256]{6,4,5,3,2,1,0:T(4,128)S(1)} %get-tuple-element.136), channel_id=1, source_target_pairs={{0,1},{1,2},{2,3},{3,4},{4,5},{5,6},{6,7},{7,8},{8,9},{9,10},{10,1... | collective-permute-start | bytes 884744 | tf_op jit(solution)/shard_map/ppermute | solution.py:20
  136.7 2.9 %collective-permute-start.8 = (f32[2,3,3,2,1,256]{5,3,4,2,1,0:T(2,128)S(1)}, f32[2,3,3,2,1,256]{5,3,4,2,1,0:T(2,128)S(1)}, u32[]{:S(2)}, u32[]{:S(2)}) collective-permute-start(f32[2,3,3,2,1,256]{5,3,4,2,1,0:T(2,128)S(1)} %fusion.127), channel_id=1, source_target_pairs={{0,15},{1,0},{2,1},{3,2},{4,3},{5,4},{6,5},{7,6},{8,7},{9,8},{10,9... | collective-permute-start | bytes 110600 | tf_op jit(solution)/shard_map/ppermute | solution.py:41
where the time goes:
time: 144 us; the launch traced here: 141 us
  other arithmetic  49 us (34%)
  waiting for transfers between devices  25 us (17%)
  local copies, waits for them, and re-layouts  24.4 us (17%)
  blocking collectives  19.5 us (14%)
  starting transfers between devices  15.8 us (11%)
  between operations  7.31 us (5%)
    all_gather x1, blocking collectives, entering(): pieces = lax.all_gather(value, axis)  19.5 us
    ppermute x4, waiting for transfers between devices, padded_2(): after = lax.ppermute(initial, axis, down)  14.7 us
    sub x175, other arithmetic, matmul_pair(): real_part + left_mat[0][:, column, None] * right_mat[0][None, column]  13.9 us
    ppermute x4, starting transfers between devices, padded_2(): after = lax.ppermute(initial, axis, down)  12.9 us
    ppermute x4, waiting for transfers between devices, padded_2(): before = lax.ppermute(last, axis, up)  8.78 us
    select_n x9, other arithmetic, yz_roll(): moved = jnp.where(inside, plain, wrapped)  7.61 us
    mul x310, local copies, waits for them, and re-layouts, matmul_pair(): left_mat[0][:, 0, None] * right_mat[0][None, 0]  4.2 us
    slice x12, local copies, waits for them, and re-layouts, yz_roll(): plain = jnp.roll(moved, -shift_z, axis=-1)  3.95 us
  transfers between devices with their start and end apart: 9, of which 7 were waited for; matrix products, arithmetic and copies ran while one was open for 2% of the time, Pallas kernels for 0%

commit v1 on v0

v1 whole, which is shorter than its diff:
```python
import functools

import jax
import jax.numpy as jnp
from jax import lax
from jax.experimental import pallas as pl
from jax.experimental.pallas import tpu as pltpu
from jax.sharding import PartitionSpec as P

MESH = pl.DeviceIdType.MESH
NZ = 16
NEWTON = 5
ape_weight = 0.4
LANES = 128


def mm(a, b, da=False, db=False):
    def left(c):
        return tuple(q[c, :, None] if da else q[:, c, None] for q in a)

    def right(c):
        return tuple(q[None, :, c] if db else q[None, c] for q in b)

    re = im = None
    for c in range(3):
        lr, li = left(c)
        rr, ri = right(c)
        x, y = lr * rr, li * ri
        u, v = lr * ri, li * rr
        re = x if re is None else re + x
        re = re + y if da != db else re - y
        if im is None:
            if da and db:
                im = -u - v
            elif da:
                im = u - v
            elif db:
                im = v - u
            else:
                im = u + v
        else:
            im = im - u if db else im + u
            im = im - v if da else im + v
    return re, im


def lane_of(shape):
    return lax.broadcasted_iota(jnp.int32, shape, len(shape) - 1)


def each(f, pair):
    return tuple(f(q) for q in pair)


def sroll(v, shift):
    shift = shift % 8
    if shift == 0:
        return v
    flat = v.reshape((9, 8, LANES))
    return pltpu.roll(flat, shift, 1).reshape(v.shape)


def lroll(v, shift):
    return pltpu.roll(v.reshape((72, LANES)), shift % LANES, 1).reshape(v.shape)


def yz_shift(pair, m, sign):
    lane = lane_of((3, 3, 8, LANES))
    z = lax.rem(lane, NZ)
    if isinstance(m, int):
        if m == 2:

            def move(v):
                r = lroll(v, -NZ * sign)
                stay = lane < LANES - NZ if sign > 0 else lane >= NZ
                return jnp.where(stay, r, sroll(r, 4))

        else:

            def move(v):
                stay = z < NZ - 1 if sign > 0 else z >= 1
                return jnp.where(stay, lroll(v, -sign), lroll(v, sign * (NZ - 1)))

        return each(move, pair)
    raise NotImplementedError


def kernel(x_ref, o_ref, U, XH, CH, PK0, PK3, acc, Q, R1, R2, GH, OUT, hs, hr, cs, cr, ds, dr, io):
    ta = lax.axis_index("ta")
    gx = lax.axis_index("gx")
    nta = lax.axis_size("ta")
    ngx = lax.axis_size("gx")

    def dev(dt, dg):
        return {"ta": lax.rem(ta + dt + nta, nta), "gx": lax.rem(gx + dg + ngx, ngx)}

    edge = (ta == 0) | (ta == 4)

    barrier = pltpu.get_barrier_semaphore()
    greeted = [dev(0, 1), dev(0, -1), dev(-1, 1), dev(1, -1)] + [dev(k, 0) for k in range(1, 8)]
    for d in greeted:
        pl.semaphore_signal(barrier, inc=1, device_id=d, device_id_type=MESH)
    for row in (0, 4):
        d = {"ta": row, "gx": lax.rem(gx + 1, ngx)}
        pl.semaphore_signal(barrier, inc=1, device_id=d, device_id_type=MESH)

    loads = []
    for t in range(2):
        for h in range(2):
            c = pltpu.make_async_copy(
                x_ref.at[:, :, :, :, t, :, pl.ds(h * LANES, LANES)],
                U.at[0, 1 + t, :, :, :, :, pl.ds(4 * h, 4), :],
                io.at[2 * t + h],
            )
            c.start()
            loads.append(c)

    def ld(ref, *at):
        v = ref[at]
        return v[0], v[1]

    def add(m, s, pair):
        acc[m, s, 0] = acc[m, s, 0] + pair[0]
        acc[m, s, 1] = acc[m, s, 1] + pair[1]

    row4 = lax.rem(lax.broadcasted_iota(jnp.int32, (3, 3, 8, LANES), 2), 4)

    def pack(w, m):
        parts = [U[w, 1, m, 0], U[w, 2, m, 0], U[w, 1, m, 1], U[w, 2, m, 1]]
        for col, out in ((0, PK0), (3, PK3)):
            moved = [sroll(v, q - col) for q, v in enumerate(parts)]
            out[w, m] = jnp.where(
                row4 < 2,
                jnp.where(row4 == 0, moved[0], moved[1]),
                jnp.where(row4 == 2, moved[2], moved[3]),
            )

    def x_next(pair, halo, t):
        return tuple(
            jnp.where(row4 == 3, sroll(halo, 3 - t - 2 * q), sroll(v, -1))
            for q, v in enumerate(pair)
        )

    def x_prev(pair, column, t):
        return tuple(
            jnp.where(row4 == 0, sroll(c, -t), sroll(v, 1)) for v, c in zip(pair, column)
        )

    def unpacked(v):
        return v, sroll(v, -2)

    def copy(w, slot, src, dst, d):
        return pltpu.make_async_remote_copy(
            src_ref=src,
            dst_ref=dst,
            send_sem=hs.at[w, slot],
            recv_sem=hr.at[w, slot],
            device_id=d,
            device_id_type=MESH,
        )

    def down(w, m):
        return copy(w, m, U.at[w, 1, m], U.at[w, 3, m], dev(-1, 0))

    def up(w, m):
        return copy(w, 4 + m, U.at[w, 2, m], U.at[w, 0, m], dev(1, 0))

    def left(w, m):
        return copy(w, 8 + m, PK0.at[w, m], XH.at[w, m], dev(0, -1))

    def right(w, m):
        return copy(w, 12 + m, PK3.at[w, m], CH.at[w, m], dev(0, 1))

    def corner_up(w):
        return copy(w, 16, PK0.at[w, 0], XH.at[w, 1], dev(1, -1))

    def corner_down(w):
        return copy(w, 17, PK3.at[w, 1], CH.at[w, 4], dev(-1, 1))

    for c in loads:
        c.wait()

    @pl.loop(0, 4)
    def _(m):
        pack(0, m)
        for s in range(2):
            acc[m, s] = 9.0 * U[0, 1 + s, m]

    pl.semaphore_wait(barrier, 11 + jnp.where(edge, 8, 0))
    corner_up(0).start()
    corner_down(0).start()
    for m in range(4):
        right(0, m).start()
        if m != 1:
            left(0, m).start()
    for m in range(4):
        up(0, m).start()
        if m != 0:
            down(0, m).start()

    def plane_yz(w):
        for s in (1, 2):
            uy, uz = ld(U, w, s, 2), ld(U, w, s, 3)
            uyz, uzy = yz_shift(uy, 3, 1), yz_shift(uz, 2, 1)
            p1, p2 = mm(uy, uzy), mm(uz, uyz)
            add(2, s - 1, mm(p2, uzy, db=True))
            add(3, s - 1, mm(p1, uyz, db=True))
            add(2, s - 1, yz_shift(mm(uz, p1, da=True), 3, -1))
            add(3, s - 1, yz_shift(mm(uy, p2, da=True), 2, -1))

    def plane_t(w, m, s):
        ut, um, umt = ld(U, w, s, 0), ld(U, w, s, m), ld(U, w, s + 1, m)
        utm = yz_shift(ut, m, 1)
        p1, p2 = mm(ut, umt), mm(um, utm)
        add(0, s - 1, mm(p2, umt, db=True))
        add(m, s - 1, mm(p1, utm, db=True))
        add(0, s - 1, yz_shift(mm(um, p1, da=True), m, -1))
        if s == 1:
            add(m, 1, mm(ut, p2, da=True))

    def plane_t_before(w, m):
        ut, um = ld(U, w, 0, 0), ld(U, w, 0, m)
        p2 = mm(um, yz_shift(ut, m, 1))
        add(m, 0, mm(ut, p2, da=True))

    def plane_tx(w):
        cx_re, cx_im = unpacked(CH[w, 1])
        far_re, far_im = unpacked(CH[w, 4])
        cx = (cx_re, cx_im)
        cxt = tuple(
            jnp.where(row4 == 0, sroll(v, -1), sroll(f, 1)) for v, f in ((cx_re, far_re), (cx_im, far_im))
        )
        ct = unpacked(CH[w, 0])
        lower_c = mm(cx, mm(ct, cxt), da=True)
        for s in (0, 1, 2):
            ut, ux = ld(U, w, s, 0), ld(U, w, s, 1)
            if s == 0:
                utx = x_next(ut, XH[w, 1], 1)
            else:
                utx = x_next(ut, XH[w, 0], s - 1)
            p2 = mm(ux, utx)
            if s < 2:
                add(1, s, mm(ut, p2, da=True))
            if s > 0:
                uxt = ld(U, w, s + 1, 1)
                p1 = mm(ut, uxt)
                add(0, s - 1, mm(p2, uxt, db=True))
                add(1, s - 1, mm(p1, utx, db=True))
                add(0, s - 1, x_prev(mm(ux, p1, da=True), lower_c, s - 1))

    def plane_x(w, m):
        cx, cm = unpacked(CH[w, 1]), unpacked(CH[w, m])
        lower_c = mm(cx, mm(cm, yz_shift(cx, m, 1)), da=True)
        for s in (1, 2):
            ux, um = ld(U, w, s, 1), ld(U, w, s, m)
            umx = x_next(um, XH[w, m], s - 1)
            uxm = yz_shift(ux, m, 1)
            p1, p2 = mm(ux, umx), mm(um, uxm)
            add(1, s - 1, mm(p2, umx, db=True))
            add(m, s - 1, mm(p1, uxm, db=True))
            add(1, s - 1, yz_shift(mm(um, p1, da=True), m, -1))
            add(m, s - 1, x_prev(mm(ux, p2, da=True), lower_c, s - 1))

    def unitarise(w, m):
        scale = ape_weight / 6.0
        for s in range(2):
            re = [[acc[m, s, 0, i, j] for j in range(3)] for i in range(3)]
            im = [[acc[m, s, 1, i, j] for j in range(3)] for i in range(3)]

            def diag(j):
                t = None
                for i in range(3):
                    q = re[i][j] * re[i][j] + im[i][j] * im[i][j]
                    t = q if t is None else t + q
                return t

            def off(j, k):
                a = b = None
                for i in range(3):
                    x = re[i][j] * re[i][k] + im[i][j] * im[i][k]
                    y = re[i][j] * im[i][k] - im[i][j] * re[i][k]
                    a = x if a is None else a + x
                    b = y if b is None else b + y
                return a, b

            k1, k2, k3 = diag(0), diag(1), diag(2)
            inverse = jnp.minimum(lax.rsqrt((scale * scale) * (k1 + k2 + k3)), 1.0)
            r = scale * inverse
            g = r * r
            a1, a2, a3 = g * k1, g * k2, g * k3
            b12 = tuple(g * v for v in off(0, 1))
            b13 = tuple(g * v for v in off(0, 2))
            b23 = tuple(g * v for v in off(1, 2))

            def norm(v):
                return v[0] * v[0] + v[1] * v[1]

            def times(a, b):
                return a[0] * b[0] - a[1] * b[1], a[0] * b[1] + a[1] * b[0]

            def ctimes(a, b):
                return a[0] * b[0] + a[1] * b[1], a[1] * b[0] - a[0] * b[1]

            j1 = a2 * a3 - norm(b23)
            j2 = a1 * a3 - norm(b13)
            j3 = a1 * a2 - norm(b12)
            q = ctimes(b13, b23)
            j12 = (q[0] - a3 * b12[0], q[1] - a3 * b12[1])
            q = times(b12, b23)
            j13 = (q[0] - a2 * b13[0], q[1] - a2 * b13[1])
            q = ctimes(b13, b12)
            j23 = (q[0] - a1 * b23[0], q[1] - a1 * b23[1])
            e1 = a1 + a2 + a3
            e2 = j1 + j2 + j3
            e3 = (
                a1 * j1
                + (b12[0] * j12[0] + b12[1] * j12[1])
                + (b13[0] * j13[0] + b13[1] * j13[1])
            )

            def reduce(d0, d1, d2, d3, d4):
                d3 = d3 + e1 * d4
                d2 = d2 - e2 * d4 + e1 * d3
                d1 = d1 + e3 * d4 - e2 * d3
                return d0 + e3 * d3, d1, d2

            h = (0.25 * e3, 2.25 - 0.25 * e2, 0.25 * e1 - 1.5)
            p = None
            for k in range(1, NEWTON):
                y = (1.5 - 0.5 * h[0], -0.5 * h[1], -0.5 * h[2])
                if p is None:
                    d3 = -0.5 * y[2]
                    p = (
                        1.5 * y[0] + e3 * d3,
                        1.5 * y[1] - 0.5 * y[0] - e2 * d3,
                        1.5 * y[2] - 0.5 * y[1] + e1 * d3,
                    )
                else:
                    p = reduce(
                        p[0] * y[0],
                        p[0] * y[1] + p[1] * y[0],
                        p[0] * y[2] + p[1] * y[1] + p[2] * y[0],
                        p[1] * y[2] + p[2] * y[1],
                        p[2] * y[2],
                    )
                if k < NEWTON - 1:
                    twice = p[0] + p[0]
                    f = reduce(
                        p[0] * p[0],
                        twice * p[1],
                        twice * p[2] + p[1] * p[1],
                        (p[1] + p[1]) * p[2],
                        p[2] * p[2],
                    )
                    h = (e3 * f[2], f[0] - e2 * f[2], f[1] + e1 * f[2])

            c2 = r * p[2]
            c1 = r * p[1] + e1 * c2
            c0 = r * p[0] - e2 * c2

            def entry(b, j):
                return c1 * b[0] + c2 * j[0], c1 * b[1] + c2 * j[1]

            m12, m13, m23 = entry(b12, j12), entry(b13, j13), entry(b23, j23)
            dg = [c0 + c1 * a + c2 * j for a, j in ((a1, j1), (a2, j2), (a3, j3))]
            table = {(0, 1): m12, (0, 2): m13, (1, 2): m23}
            for i in range(3):
                for j in range(3):
                    x = re[i][j] * dg[j]
                    y = im[i][j] * dg[j]
                    for k in range(3):
                        if k == j:
                            continue
                        vr, vi = table[(min(k, j), max(k, j))]
                        ur, ui = re[i][k], im[i][k]
                        if k < j:
                            x = x + ur * vr - ui * vi
                            y = y + ur * vi + ui * vr
                        else:
                            x = x + ur * vr + ui * vi
                            y = y - ur * vi + ui * vr
                    U[w + 1, 1 + s, m, 0, i, j] = x
                    U[w + 1, 1 + s, m, 1, i, j] = y
        for s in range(2):
            acc[m, s] = 9.0 * U[w + 1, 1 + s, m]

    def scatter(stage, src, dst, k):
        return pltpu.make_async_remote_copy(
            src_ref=src.at[:, :, :, pl.ds(k, 1), :],
            dst_ref=dst.at[:, :, :, pl.ds(8 - k, 1), :],
            send_sem=cs.at[stage, k],
            recv_sem=cr.at[stage, 8 - k],
            device_id=dev(k, 0),
            device_id_type=MESH,
        )

    def gathered(stage, src, dst, k):
        return pltpu.make_async_remote_copy(
            src_ref=src.at[:, :, :, pl.ds(8 - k, 1), :],
            dst_ref=dst.at[:, :, :, pl.ds(k, 1), :],
            send_sem=cs.at[stage, 8 - k],
            recv_sem=cr.at[stage, k],
            device_id=dev(8 - k, 0),
            device_id_type=MESH,
        )

    def turn(v, shift):
        flat = v.reshape((9, 8, LANES))
        return pltpu.roll(flat, shift, 1).reshape(v.shape)

    back = lax.rem(8 - ta, 8)

    def chain_start():
        q = mm(ld(U, 2, 1, 0), ld(U, 2, 2, 0))
        for c in range(2):
            Q[0, c] = turn(q[c], back)
        for k in range(1, 8):
            scatter(0, Q.at[0], R1, k).start()

    @pl.loop(0, 2)
    def _(w):
        plane_yz(w)
        for m in (2, 3):
            plane_t(w, m, 1)
        for m in (1, 2, 3):
            down(w, m).wait_recv()
        for m in range(4):
            up(w, m).wait_recv()
        for m in (2, 3):
            plane_t(w, m, 2)
            plane_t_before(w, m)
        for m in range(4):
            if m != 1:
                left(w, m).wait_recv()
            right(w, m).wait_recv()
        corner_up(w).wait_recv()
        corner_down(w).wait_recv()
        plane_tx(w)
        unitarise(w, 0)
        pack(w + 1, 0)
        left(w + 1, 0).start()

        @pl.when(w == 0)
        def _():
            corner_up(1).start()
            right(1, 0).start()
            up(1, 0).start()

        @pl.when(w == 1)
        def _():
            chain_start()

        for m in (2, 3):
            plane_x(w, m)

        @pl.loop(1, 4)
        def _(m):
            unitarise(w, m)

            @pl.when(w == 0)
            def _():
                pack(1, m)
                right(1, m).start()

                @pl.when(m != 1)
                def _():
                    left(1, m).start()

                @pl.when(m == 1)
                def _():
                    corner_down(1).start()

                up(1, m).start()
                down(1, m).start()

    for k in range(1, 8):
        gathered(0, Q.at[0], R1, k).wait_recv()
    sub = lax.broadcasted_iota(jnp.int32, (3, 3, 8, LANES), 2)
    eye = (
        lax.broadcasted_iota(jnp.int32, (3, 3, 8, LANES), 0)
        == lax.broadcasted_iota(jnp.int32, (3, 3, 8, LANES), 1)
    ).astype(jnp.float32)
    run = tuple(turn(jnp.where(sub == 0, Q[0, c], R1[c]), ta) for c in range(2))
    for step in (1, 2, 4):
        joined = mm(each(lambda v: sroll(v, step), run), run)
        run = tuple(jnp.where(sub >= step, j, v) for j, v in zip(joined, run))
    entering = (
        jnp.where(sub == 0, eye, sroll(run[0], 1)),
        jnp.where(sub == 0, 0.0, sroll(run[1], 1)),
    )
    for c in range(2):
        Q[1, c] = turn(entering[c], back)

    def column(k, h):
        return pltpu.make_async_remote_copy(
            src_ref=Q.at[1, :, :, :, pl.ds(k, 1), :],
            dst_ref=GH.at[:, :, :, pl.ds(4 * h + 3, 1), :],
            send_sem=ds.at[k],
            recv_sem=dr.at[h],
            device_id=dev(k, -1),
            device_id_type=MESH,
        )

    for h in range(2):

        @pl.when(ta == 4 * h)
        def _():
            for k in range(8):
                column(k, h).start()

    for k in range(1, 8):
        scatter(1, Q.at[1], R2, k).start()

    for k in range(1, 8):
        gathered(1, Q.at[1], R2, k).wait_recv()
    g1 = tuple(turn(jnp.where(sub == 0, Q[1, c], R2[c]), ta) for c in range(2))
    g2 = mm(g1, ld(U, 2, 1, 0))
    g3 = mm(g2, ld(U, 2, 2, 0))
    gs = (g1, g2)

    def store(m, s, pair):
        OUT[m, 0, :, :, s] = pair[0]
        OUT[m, 1, :, :, s] = pair[1]

    def save(m, t, h):
        return pltpu.make_async_copy(
            OUT.at[m, :, :, :, t, pl.ds(4 * h, 4), :],
            o_ref.at[m, :, :, :, t, :, pl.ds(h * LANES, LANES)],
            io.at[4 * m + 2 * t + h],
        )

    def save_all(m):
        for t in range(2):
            for h in range(2):
                save(m, t, h).start()

    store(0, 0, mm(g2, g2, db=True))
    store(0, 1, mm(g3, g3, db=True))
    save_all(0)
    for m in (2, 3):
        for s in range(2):
            store(m, s, mm(mm(gs[s], ld(U, 2, 1 + s, m)), yz_shift(gs[s], m, 1), db=True))
        save_all(m)
    left(2, 0).wait_recv()
    for h in range(2):
        pltpu.make_async_remote_copy(
            src_ref=Q.at[1, :, :, :, pl.ds(0, 1), :],
            dst_ref=GH.at[:, :, :, pl.ds(4 * h + 3, 1), :],
            send_sem=ds.at[0],
            recv_sem=dr.at[h],
            device_id=dev(0, -1),
            device_id_type=MESH,
        ).wait_recv()
    halo = XH[2, 0]
    gh1 = (GH[0], GH[1])
    gh2 = mm(gh1, tuple(sroll(halo, 3 - 2 * q) for q in range(2)))
    for s, gh in ((0, gh1), (1, gh2)):
        gx_next = tuple(jnp.where(row4 == 3, a, sroll(b, -1)) for a, b in zip(gh, gs[s]))
        store(1, s, mm(mm(gs[s], ld(U, 2, 1 + s, 1)), gx_next, db=True))
    save_all(1)

    for w in range(2):
        for m in range(4):
            if m != 0:
                down(w, m).wait_send()
            up(w, m).wait_send()
            if m != 1:
                left(w, m).wait_send()
            right(w, m).wait_send()
        corner_up(w).wait_send()
        corner_down(w).wait_send()
    left(2, 0).wait_send()
    for k in range(1, 8):
        scatter(0, Q.at[0], R1, k).wait_send()
        scatter(1, Q.at[1], R2, k).wait_send()
    for h in range(2):

        @pl.when(ta == 4 * h)
        def _():
            for k in range(8):
                column(k, h).wait_send()

    for m in range(4):
        for t in range(2):
            for h in range(2):
                save(m, t, h).wait()


def body(gauge_links):
    field = (2, 3, 3, 8, LANES)
    f32 = jnp.float32
    return pl.pallas_call(
        kernel,
        out_shape=jax.ShapeDtypeStruct(gauge_links.shape, f32),
        in_specs=[pl.BlockSpec(memory_space=pl.ANY)],
        out_specs=pl.BlockSpec(memory_space=pl.ANY),
        scratch_shapes=[
            pltpu.VMEM((3, 4, 4) + field, f32),
            pltpu.VMEM((3, 4) + field[1:], f32),
            pltpu.VMEM((2, 5) + field[1:], f32),
            pltpu.VMEM((3, 4) + field[1:], f32),
            pltpu.VMEM((3, 4) + field[1:], f32),
            pltpu.VMEM((4, 2) + field, f32),
            pltpu.VMEM((2,) + field, f32),
            pltpu.VMEM(field, f32),
            pltpu.VMEM(field, f32),
            pltpu.VMEM(field, f32),
            pltpu.VMEM((4, 2, 3, 3, 2, 8, LANES), f32),
            pltpu.SemaphoreType.DMA((3, 18)),
            pltpu.SemaphoreType.DMA((3, 18)),
            pltpu.SemaphoreType.DMA((2, 8)),
            pltpu.SemaphoreType.DMA((2, 8)),
            pltpu.SemaphoreType.DMA((8,)),
            pltpu.SemaphoreType.DMA((2,)),
            pltpu.SemaphoreType.DMA((16,)),
        ],
        compiler_params=pltpu.CompilerParams(
            collective_id=0, has_side_effects=True, vmem_limit_bytes=32 * 2**20
        ),
    )(gauge_links)


def solution(mesh):
    spec = P(None, None, None, None, "ta", "gx", None)
    return jax.shard_map(body, mesh=mesh, in_specs=(spec,), out_specs=spec, check_vma=False)
```

time: 144 us -> 36.1 us (0.25); the launches traced: 141 us -> 35.9 us
  other arithmetic: 49 us -> 0 us
  Pallas kernels: 0 us -> 34.1 us
  waiting for transfers between devices: 25 us -> 0 us
  local copies, waits for them, and re-layouts: 24.4 us -> 1.88 us
  blocking collectives: 19.5 us -> 0 us
  starting transfers between devices: 15.8 us -> 0 us
  between operations: 7.31 us -> 0.01 us
    pallas_call x0 -> x1, Pallas kernels: none -> 34.1 us  [body(): pl.pallas_call(kernel, out_shape=jax.ShapeDtypeStruct(gauge_links.shape,...]
    ppermute x9 -> x0, waiting for transfers between devices: 25 us -> none  [the longest x4 14.7 us: padded_2(): after = lax.ppermute(initial, axis, down)]
    all_gather x1 -> x0, blocking collectives: 19.5 us -> none  [entering(): pieces = lax.all_gather(value, axis)]
    sub x203 -> x0, other arithmetic: 17.6 us -> none  [the longest x175 13.9 us: matmul_pair(): real_part + left_mat[0][:, column, None] * right_mat[0][None, column]]
    ppermute x9 -> x0, starting transfers between devices: 15.8 us -> none  [the longest x4 12.9 us: padded_2(): after = lax.ppermute(initial, axis, down)]
    slice x40 -> x0, local copies, waits for them, and re-layouts: 13.3 us -> none  [the longest x12 3.95 us: yz_roll(): plain = jnp.roll(moved, -shift_z, axis=-1)]
    select_n x16 -> x0, other arithmetic: 8.15 us -> none  [the longest x9 7.61 us: yz_roll(): moved = jnp.where(inside, plain, wrapped)]
    mul x68 -> x0, other arithmetic: 7.04 us -> none  [the longest x22 3.8 us: matmul_pair(): left_mat[0][:, 0, None] * right_mat[0][None, 0]]
  transfers between devices with their start and end apart: 9 -> 0, of which waited for: 7 -> 0; matrix products, arithmetic and copies ran while one was open for 2% -> 0% of each run, Pallas kernels for 0% -> 0%
where the time goes in v1:
time: 36.1 us; the launch traced here: 35.9 us
  Pallas kernels  34.1 us (94%)
  local copies, waits for them, and re-layouts  1.88 us (5%)
    pallas_call x1, Pallas kernels, body(): pl.pallas_call(kernel, out_shape=jax.ShapeDtypeStruct(gauge_links.shape,...  34.1 us
    unnamed x3, local copies, waits for them, and re-layouts  1.88 us

profile of v1, /device:TPU:1, one launch (start us, length us, event | category | flops | bytes accessed | tf_op | source)
XLA Modules:
  0.0 35.9 jit_solution(11048999720633430116)
XLA Ops:
  0.0 0.0 copy-start
  0.0 1.1 %copy-done = f32[4,2,3,3,2,4,256]{6,5,4,3,2,1,0:T(4,128)S(1)} copy-done((f32[4,2,3,3,2,4,256]{6,5,4,3,2,1,0:T(4,128)S(1)}, f32[4,2,3,3,2,4,256]{6,5,4,3,2,1,0:T(4,128)}, u32[]{:S(2)}) %copy-start) | copy-done | bytes 589848
  1.1 34.1 %shard_map.17 = f32[4,2,3,3,2,4,256]{6,5,4,3,2,1,0:T(4,128)S(1)} custom-call(f32[4,2,3,3,2,4,256]{6,5,4,3,2,1,0:T(4,128)S(1)} %copy-done), custom_call_target="tpu_custom_call" | custom-call | tf_op jit(solution)/shard_map/pallas_call | solution.py:592
  35.1 0.8 %copy.3 = f32[4,2,3,3,2,4,256]{6,5,4,3,2,1,0:T(4,128)} copy(f32[4,2,3,3,2,4,256]{6,5,4,3,2,1,0:T(4,128)S(1)} %shard_map.17) | data formatting | bytes 1179648
Async XLA Ops:
  0.0 1.1 %copy-start = (f32[4,2,3,3,2,4,256]{6,5,4,3,2,1,0:T(4,128)S(1)}, f32[4,2,3,3,2,4,256]{6,5,4,3,2,1,0:T(4,128)}, u32[]{:S(2)}) copy-start(f32[4,2,3,3,2,4,256]{6,5,4,3,2,1,0:T(4,128)} %x_ref.1) | copy-start | bytes 1769476

commit v2 on v1

--- a/solution.py
+++ b/solution.py
@@ -94,14 +94,9 @@
     def dev(dt, dg):
         return {"ta": lax.rem(ta + dt + nta, nta), "gx": lax.rem(gx + dg + ngx, ngx)}
 
-    edge = (ta == 0) | (ta == 4)
-
     barrier = pltpu.get_barrier_semaphore()
     greeted = [dev(0, 1), dev(0, -1), dev(-1, 1), dev(1, -1)] + [dev(k, 0) for k in range(1, 8)]
     for d in greeted:
-        pl.semaphore_signal(barrier, inc=1, device_id=d, device_id_type=MESH)
-    for row in (0, 4):
-        d = {"ta": row, "gx": lax.rem(gx + 1, ngx)}
         pl.semaphore_signal(barrier, inc=1, device_id=d, device_id_type=MESH)
 
     loads = []
@@ -186,7 +181,7 @@
         for s in range(2):
             acc[m, s] = 9.0 * U[0, 1 + s, m]
 
-    pl.semaphore_wait(barrier, 11 + jnp.where(edge, 8, 0))
+    pl.semaphore_wait(barrier, 11)
     corner_up(0).start()
     corner_down(0).start()
     for m in range(4):
@@ -592,7 +587,7 @@
     return pl.pallas_call(
         kernel,
         out_shape=jax.ShapeDtypeStruct(gauge_links.shape, f32),
-        in_specs=[pl.BlockSpec(memory_space=pl.ANY)],
+        in_specs=[pl.BlockSpec(memory_space=pltpu.HBM)],
         out_specs=pl.BlockSpec(memory_space=pl.ANY),
         scratch_shapes=[
             pltpu.VMEM((3, 4, 4) + field, f32),

time: 36.1 us -> 36.3 us (level)
  no operation moved by 1% of the time
where the time goes in v2:
time: 36.3 us; the launch traced here: 36.1 us
  Pallas kernels  34.2 us (94%)
  local copies, waits for them, and re-layouts  1.88 us (5%)
    pallas_call x1, Pallas kernels, body(): pl.pallas_call(kernel, out_shape=jax.ShapeDtypeStruct(gauge_links.shape,...  34.2 us
    unnamed x3, local copies, waits for them, and re-layouts  1.88 us

profile of v2, /device:TPU:1, one launch (start us, length us, event | category | flops | bytes accessed | tf_op | source)
XLA Modules:
  0.0 36.1 jit_solution(17671495686162571864)
XLA Ops:
  0.0 0.0 copy-start
  0.0 1.1 %copy-done = f32[4,2,3,3,2,4,256]{6,5,4,3,2,1,0:T(4,128)S(1)} copy-done((f32[4,2,3,3,2,4,256]{6,5,4,3,2,1,0:T(4,128)S(1)}, f32[4,2,3,3,2,4,256]{6,5,4,3,2,1,0:T(4,128)}, u32[]{:S(2)}) %copy-start) | copy-done | bytes 589848
  1.1 34.2 %shard_map.17 = f32[4,2,3,3,2,4,256]{6,5,4,3,2,1,0:T(4,128)S(1)} custom-call(f32[4,2,3,3,2,4,256]{6,5,4,3,2,1,0:T(4,128)S(1)} %copy-done), custom_call_target="tpu_custom_call" | custom-call | tf_op jit(solution)/shard_map/pallas_call | solution.py:587
  35.3 0.8 %copy.3 = f32[4,2,3,3,2,4,256]{6,5,4,3,2,1,0:T(4,128)} copy(f32[4,2,3,3,2,4,256]{6,5,4,3,2,1,0:T(4,128)S(1)} %shard_map.17) | data formatting | bytes 1179648
Async XLA Ops:
  0.0 1.1 %copy-start = (f32[4,2,3,3,2,4,256]{6,5,4,3,2,1,0:T(4,128)S(1)}, f32[4,2,3,3,2,4,256]{6,5,4,3,2,1,0:T(4,128)}, u32[]{:S(2)}) copy-start(f32[4,2,3,3,2,4,256]{6,5,4,3,2,1,0:T(4,128)} %x_ref.1) | copy-start | bytes 1769476

commit v3 on v2

--- a/solution.py
+++ b/solution.py
@@ -85,18 +85,20 @@
     raise NotImplementedError
 
 
-def kernel(x_ref, o_ref, U, XH, CH, PK0, PK3, acc, Q, R1, R2, GH, OUT, hs, hr, cs, cr, ds, dr, io):
+def kernel(
+    x_ref, o_ref, U, XH, CH, PK0, PK3, RL, acc, Q, SQ, CQ, EH, XQ, OUT, hs, hr, cs, cr, io
+):
     ta = lax.axis_index("ta")
     gx = lax.axis_index("gx")
     nta = lax.axis_size("ta")
     ngx = lax.axis_size("gx")
+    core, chip = lax.rem(ta, 2), ta // 2
 
     def dev(dt, dg):
         return {"ta": lax.rem(ta + dt + nta, nta), "gx": lax.rem(gx + dg + ngx, ngx)}
 
     barrier = pltpu.get_barrier_semaphore()
-    greeted = [dev(0, 1), dev(0, -1), dev(-1, 1), dev(1, -1)] + [dev(k, 0) for k in range(1, 8)]
-    for d in greeted:
+    for d in (dev(0, 1), dev(0, -1), dev(4, 0), dev(1, 0), dev(-1, 0)):
         pl.semaphore_signal(barrier, inc=1, device_id=d, device_id_type=MESH)
 
     loads = []
@@ -154,23 +156,64 @@
             device_id_type=MESH,
         )
 
+    def face(w, s, m):
+        return U.at[w, s, m, :, pl.ds(0, 2)] if w == 0 else U.at[w, s, m]
+
+    def cols(ref, w, m):
+        return ref.at[w, m, pl.ds(0, 2)] if w == 0 else ref.at[w, m]
+
     def down(w, m):
-        return copy(w, m, U.at[w, 1, m], U.at[w, 3, m], dev(-1, 0))
+        return copy(w, m, face(w, 1, m), face(w, 3, m), dev(-1, 0))
 
     def up(w, m):
-        return copy(w, 4 + m, U.at[w, 2, m], U.at[w, 0, m], dev(1, 0))
+        return copy(w, 4 + m, face(w, 2, m), face(w, 0, m), dev(1, 0))
 
     def left(w, m):
-        return copy(w, 8 + m, PK0.at[w, m], XH.at[w, m], dev(0, -1))
+        return copy(w, 8 + m, cols(PK0, w, m), cols(XH, w, m), dev(0, -1))
 
     def right(w, m):
-        return copy(w, 12 + m, PK3.at[w, m], CH.at[w, m], dev(0, 1))
+        return copy(w, 12 + m, cols(PK3, w, m), cols(CH, w, m), dev(0, 1))
 
     def corner_up(w):
-        return copy(w, 16, PK0.at[w, 0], XH.at[w, 1], dev(1, -1))
+        return copy(w, 16, cols(PK0, w, 0), cols(XH, w, 1), dev(1, -1))
 
     def corner_down(w):
-        return copy(w, 17, PK3.at[w, 1], CH.at[w, 4], dev(-1, 1))
+        return copy(w, 17, cols(PK3, w, 1), cols(CH, w, 4), dev(-1, 1))
+
+    def first_up():
+        return copy(0, 18, cols(PK0, 0, 0), RL.at[0], dev(1, 0))
+
+    def first_down():
+        return copy(0, 19, cols(PK3, 0, 1), RL.at[1], dev(-1, 0))
+
+    def then_left():
+        return copy(0, 16, RL.at[0], cols(XH, 0, 1), dev(0, -1))
+
+    def then_right():
+        return copy(0, 17, RL.at[1], cols(CH, 0, 4), dev(0, 1))
+
+    def cross(a, b):
+        out = []
+        for j in range(3):
+            (pr, pi), (qr, qi) = a[(j + 1) % 3], b[(j + 2) % 3]
+            (tr, ti), (ur, ui) = a[(j + 2) % 3], b[(j + 1) % 3]
+            out.append((pr * qr - pi * qi - tr * ur + ti * ui, tr * ui + ti * ur - pr * qi - pi * qr))
+        return out
+
+    def third_face(s, m):
+        rows = [[(U[0, s, m, 0, i, j], U[0, s, m, 1, i, j]) for j in range(3)] for i in range(2)]
+        for j, (re, im) in enumerate(cross(*rows)):
+            U[0, s, m, 0, 2, j] = re
+            U[0, s, m, 1, 2, j] = im
+
+    quad = lax.rem(lax.broadcasted_iota(jnp.int32, (8, LANES), 0), 4)
+
+    def third_cols(ref, m):
+        rows = [
+            [(ref[0, m, i, j], pltpu.roll(ref[0, m, i, j], 6, 0)) for j in range(3)] for i in range(2)
+        ]
+        for j, (re, im) in enumerate(cross(*rows)):
+            ref[0, m, 2, j] = jnp.where(quad < 2, re, pltpu.roll(im, 2, 0))
 
     for c in loads:
         c.wait()
@@ -181,10 +224,10 @@
         for s in range(2):
             acc[m, s] = 9.0 * U[0, 1 + s, m]
 
-    pl.semaphore_wait(barrier, 11)
-    corner_up(0).start()
-    corner_down(0).start()
-    for m in range(4):
+    pl.semaphore_wait(barrier, 5)
+    first_down().start()
+    first_up().start()
+    for m in (1, 0, 2, 3):
         right(0, m).start()
         if m != 1:
             left(0, m).start()
@@ -379,136 +422,179 @@
         for s in range(2):
             acc[m, s] = 9.0 * U[w + 1, 1 + s, m]
 
-    def scatter(stage, src, dst, k):
-        return pltpu.make_async_remote_copy(
-            src_ref=src.at[:, :, :, pl.ds(k, 1), :],
-            dst_ref=dst.at[:, :, :, pl.ds(8 - k, 1), :],
-            send_sem=cs.at[stage, k],
-            recv_sem=cr.at[stage, 8 - k],
-            device_id=dev(k, 0),
-            device_id_type=MESH,
-        )
-
-    def gathered(stage, src, dst, k):
-        return pltpu.make_async_remote_copy(
-            src_ref=src.at[:, :, :, pl.ds(8 - k, 1), :],
-            dst_ref=dst.at[:, :, :, pl.ds(k, 1), :],
-            send_sem=cs.at[stage, 8 - k],
-            recv_sem=cr.at[stage, k],
-            device_id=dev(8 - k, 0),
-            device_id_type=MESH,
-        )
-
-    def turn(v, shift):
-        flat = v.reshape((9, 8, LANES))
-        return pltpu.roll(flat, shift, 1).reshape(v.shape)
-
-    back = lax.rem(8 - ta, 8)
-
-    def chain_start():
-        q = mm(ld(U, 2, 1, 0), ld(U, 2, 2, 0))
-        for c in range(2):
-            Q[0, c] = turn(q[c], back)
-        for k in range(1, 8):
-            scatter(0, Q.at[0], R1, k).start()
-
-    @pl.loop(0, 2)
-    def _(w):
-        plane_yz(w)
-        for m in (2, 3):
-            plane_t(w, m, 1)
-        for m in (1, 2, 3):
-            down(w, m).wait_recv()
-        for m in range(4):
-            up(w, m).wait_recv()
-        for m in (2, 3):
-            plane_t(w, m, 2)
-            plane_t_before(w, m)
-        for m in range(4):
-            if m != 1:
-                left(w, m).wait_recv()
-            right(w, m).wait_recv()
-        corner_up(w).wait_recv()
-        corner_down(w).wait_recv()
-        plane_tx(w)
-        unitarise(w, 0)
-        pack(w + 1, 0)
-        left(w + 1, 0).start()
-
-        @pl.when(w == 0)
-        def _():
-            corner_up(1).start()
-            right(1, 0).start()
-            up(1, 0).start()
-
-        @pl.when(w == 1)
-        def _():
-            chain_start()
-
-        for m in (2, 3):
-            plane_x(w, m)
-
-        @pl.loop(1, 4)
-        def _(m):
-            unitarise(w, m)
-
-            @pl.when(w == 0)
-            def _():
-                pack(1, m)
-                right(1, m).start()
-
-                @pl.when(m != 1)
-                def _():
-                    left(1, m).start()
-
-                @pl.when(m == 1)
-                def _():
-                    corner_down(1).start()
-
-                up(1, m).start()
-                down(1, m).start()
-
-    for k in range(1, 8):
-        gathered(0, Q.at[0], R1, k).wait_recv()
     sub = lax.broadcasted_iota(jnp.int32, (3, 3, 8, LANES), 2)
     eye = (
         lax.broadcasted_iota(jnp.int32, (3, 3, 8, LANES), 0)
         == lax.broadcasted_iota(jnp.int32, (3, 3, 8, LANES), 1)
     ).astype(jnp.float32)
-    run = tuple(turn(jnp.where(sub == 0, Q[0, c], R1[c]), ta) for c in range(2))
-    for step in (1, 2, 4):
-        joined = mm(each(lambda v: sroll(v, step), run), run)
-        run = tuple(jnp.where(sub >= step, j, v) for j, v in zip(joined, run))
-    entering = (
-        jnp.where(sub == 0, eye, sroll(run[0], 1)),
-        jnp.where(sub == 0, 0.0, sroll(run[1], 1)),
-    )
-    for c in range(2):
-        Q[1, c] = turn(entering[c], back)
-
-    def column(k, h):
+    one = (eye, jnp.zeros_like(eye))
+    lower = core == 0
+    sibling = dev(1 - 2 * core, 0)
+
+    def pick(cond, a, b):
+        return tuple(jnp.where(cond, x, y) for x, y in zip(a, b))
+
+    def chain_copy(slot, src, dst, d):
         return pltpu.make_async_remote_copy(
-            src_ref=Q.at[1, :, :, :, pl.ds(k, 1), :],
-            dst_ref=GH.at[:, :, :, pl.ds(4 * h + 3, 1), :],
-            send_sem=ds.at[k],
-            recv_sem=dr.at[h],
-            device_id=dev(k, -1),
+            src_ref=src,
+            dst_ref=dst,
+            send_sem=cs.at[slot],
+            recv_sem=cr.at[slot],
+            device_id=d,
             device_id_type=MESH,
         )
 
-    for h in range(2):
-
-        @pl.when(ta == 4 * h)
+    def rows(ref, first, count):
+        return ref.at[:, :, :, pl.ds(first, count), :]
+
+    def to_sibling():
+        return chain_copy(0, Q.at[0], SQ, sibling)
+
+    def half_to(k):
+        return chain_copy(k, rows(Q.at[1], 0, 4), rows(CQ.at[k - 1], 0, 4), dev(2 * k, 0))
+
+    def column_to(k, h):
+        return chain_copy(
+            2 + 2 * k + h, rows(Q.at[2], 4 * h, 1), rows(CQ.at[k - 1], 4 + h, 1), dev(2 * k, -1)
+        )
+
+    def column_own(h):
+        return chain_copy(10 + h, rows(Q.at[0], 4 * h, 1), rows(XQ, 4 * h + 3, 1), dev(1, -1))
+
+    def entering_to_sibling():
+        return chain_copy(12, rows(Q.at[3], 0, 4), rows(EH, 4, 4), sibling)
+
+    def chain_start():
+        q = mm(ld(U, 2, 1, 0), ld(U, 2, 2, 0))
+        Q[0, 0] = q[0]
+        Q[0, 1] = q[1]
+        to_sibling().start()
+
+        @pl.when(lower)
         def _():
-            for k in range(8):
-                column(k, h).start()
-
-    for k in range(1, 8):
-        scatter(1, Q.at[1], R2, k).start()
-
-    for k in range(1, 8):
-        gathered(1, Q.at[1], R2, k).wait_recv()
-    g1 = tuple(turn(jnp.where(sub == 0, Q[1, c], R2[c]), ta) for c in range(2))
+            for h in range(2):
+                column_own(h).start()
+
+    def chain_middle():
+        to_sibling().wait_recv()
+        mine, other = ld(Q, 0), (SQ[0], SQ[1])
+        q = mm(pick(lower, mine, other), pick(lower, other, mine))
+        for c in range(2):
+            Q[2, c] = q[c]
+            Q[1, c] = jnp.where(lower, q[c], sroll(q[c], 4))
+        for k in (1, 3, 2):
+
+            @pl.when(chip + k < 4)
+            def _():
+                half_to(k).start()
+                for h in range(2):
+                    column_to(k, h).start()
+
+    def sweep_start(w):
+        plane_yz(w)
+        for m in (2, 3):
+            plane_t(w, m, 1)
+
+    def sweep_time(w):
+        for m in (2, 3):
+            plane_t(w, m, 2)
+            plane_t_before(w, m)
+
+    def wait_time(w):
+        for m in range(4):
+            up(w, m).wait_recv()
+            if m != 0:
+                down(w, m).wait_recv()
+
+    def wait_x(w):
+        for m in range(4):
+            right(w, m).wait_recv()
+            if m != 1:
+                left(w, m).wait_recv()
+
+    sweep_start(0)
+    first_down().wait_recv()
+    then_right().start()
+    first_up().wait_recv()
+    then_left().start()
+    wait_time(0)
+    for m in range(4):
+        third_face(0, m)
+        if m != 0:
+            third_face(3, m)
+    sweep_time(0)
+    wait_x(0)
+    for m in range(4):
+        third_cols(CH, m)
+        if m != 1:
+            third_cols(XH, m)
+    for m in (2, 3):
+        plane_x(0, m)
+    then_left().wait_recv()
+    then_right().wait_recv()
+    third_cols(XH, 1)
+    third_cols(CH, 4)
+    plane_tx(0)
+    for m in range(4):
+        unitarise(0, m)
+        pack(1, m)
+        if m == 0:
+            corner_up(1).start()
+        if m == 1:
+            corner_down(1).start()
+        right(1, m).start()
+        if m != 1:
+            left(1, m).start()
+        up(1, m).start()
+        if m != 0:
+            down(1, m).start()
+
+    sweep_start(1)
+    wait_time(1)
+    sweep_time(1)
+    wait_x(1)
+    corner_up(1).wait_recv()
+    corner_down(1).wait_recv()
+    plane_tx(1)
+    unitarise(1, 0)
+    chain_start()
+    pack(2, 0)
+    left(2, 0).start()
+    for m in (2, 3):
+        plane_x(1, m)
+    chain_middle()
+    for m in (1, 2, 3):
+        unitarise(1, m)
+
+    for k in (1, 2, 3):
+
+        @pl.when(chip >= k)
+        def _():
+            half_to(k).wait_recv()
+            for h in range(2):
+                column_to(k, h).wait_recv()
+
+    run = pick(chip >= 3, ld(CQ, 2), one)
+    run = pick(chip >= 2, mm(run, ld(CQ, 1)), one)
+    run = pick(chip >= 1, mm(run, ld(CQ, 0)), one)
+    for c in range(2):
+        Q[3, c] = run[c]
+    entering_to_sibling().start()
+    gh1 = tuple(jnp.where(sub < 4, sroll(v, -1), sroll(v, 2)) for v in run)
+
+    @pl.when(core == 1)
+    def _():
+        for h in range(2):
+            chain_copy(10 + h, rows(Q.at[0], 4 * h, 1), rows(XQ, 4 * h + 3, 1), dev(1, -1)).wait_recv()
+
+    gh1 = pick(lower, gh1, mm(gh1, (XQ[0], XQ[1])))
+    left(2, 0).wait_recv()
+    halo = XH[2, 0]
+    gh2 = mm(gh1, tuple(sroll(halo, 3 - 2 * q) for q in range(2)))
+    entering_to_sibling().wait_recv()
+    whole = tuple(jnp.where(sub < 4, v, EH[c]) for c, v in enumerate(run))
+    whole = pick(lower, whole, each(lambda v: sroll(v, 4), whole))
+    g1 = pick(lower, whole, mm(whole, (SQ[0], SQ[1])))
     g2 = mm(g1, ld(U, 2, 1, 0))
     g3 = mm(g2, ld(U, 2, 2, 0))
     gs = (g1, g2)
@@ -536,19 +622,6 @@
         for s in range(2):
             store(m, s, mm(mm(gs[s], ld(U, 2, 1 + s, m)), yz_shift(gs[s], m, 1), db=True))
         save_all(m)
-    left(2, 0).wait_recv()
-    for h in range(2):
-        pltpu.make_async_remote_copy(
-            src_ref=Q.at[1, :, :, :, pl.ds(0, 1), :],
-            dst_ref=GH.at[:, :, :, pl.ds(4 * h + 3, 1), :],
-            send_sem=ds.at[0],
-            recv_sem=dr.at[h],
-            device_id=dev(0, -1),
-            device_id_type=MESH,
-        ).wait_recv()
-    halo = XH[2, 0]
-    gh1 = (GH[0], GH[1])
-    gh2 = mm(gh1, tuple(sroll(halo, 3 - 2 * q) for q in range(2)))
     for s, gh in ((0, gh1), (1, gh2)):
         gx_next = tuple(jnp.where(row4 == 3, a, sroll(b, -1)) for a, b in zip(gh, gs[s]))
         store(1, s, mm(mm(gs[s], ld(U, 2, 1 + s, 1)), gx_next, db=True))
@@ -562,18 +635,29 @@
             if m != 1:
                 left(w, m).wait_send()
             right(w, m).wait_send()
-        corner_up(w).wait_send()
-        corner_down(w).wait_send()
+        if w == 1:
+            corner_up(w).wait_send()
+            corner_down(w).wait_send()
+    first_up().wait_send()
+    first_down().wait_send()
+    then_left().wait_send()
+    then_right().wait_send()
     left(2, 0).wait_send()
-    for k in range(1, 8):
-        scatter(0, Q.at[0], R1, k).wait_send()
-        scatter(1, Q.at[1], R2, k).wait_send()
-    for h in range(2):
-
-        @pl.when(ta == 4 * h)
+    to_sibling().wait_send()
+    entering_to_sibling().wait_send()
+
+    @pl.when(lower)
+    def _():
+        for h in range(2):
+            column_own(h).wait_send()
+
+    for k in (1, 2, 3):
+
+        @pl.when(chip + k < 4)
         def _():
-            for k in range(8):
-                column(k, h).wait_send()
+            half_to(k).wait_send()
+            for h in range(2):
+                column_to(k, h).wait_send()
 
     for m in range(4):
         for t in range(2):
@@ -595,18 +679,18 @@
             pltpu.VMEM((2, 5) + field[1:], f32),
             pltpu.VMEM((3, 4) + field[1:], f32),
             pltpu.VMEM((3, 4) + field[1:], f32),
+            pltpu.VMEM((2, 2) + field[2:], f32),
             pltpu.VMEM((4, 2) + field, f32),
-            pltpu.VMEM((2,) + field, f32),
+            pltpu.VMEM((4,) + field, f32),
             pltpu.VMEM(field, f32),
+            pltpu.VMEM((3,) + field, f32),
             pltpu.VMEM(field, f32),
             pltpu.VMEM(field, f32),
             pltpu.VMEM((4, 2, 3, 3, 2, 8, LANES), f32),
-            pltpu.SemaphoreType.DMA((3, 18)),
-            pltpu.SemaphoreType.DMA((3, 18)),
-            pltpu.SemaphoreType.DMA((2, 8)),
-            pltpu.SemaphoreType.DMA((2, 8)),
-            pltpu.SemaphoreType.DMA((8,)),
-            pltpu.SemaphoreType.DMA((2,)),
+            pltpu.SemaphoreType.DMA((3, 20)),
+            pltpu.SemaphoreType.DMA((3, 20)),
+            pltpu.SemaphoreType.DMA((13,)),
+            pltpu.SemaphoreType.DMA((13,)),
             pltpu.SemaphoreType.DMA((16,)),
         ],
         compiler_params=pltpu.CompilerParams(

time: 36.3 us -> 32.1 us (0.88)
  the two profiles are of different devices: /device:TPU:1 before, /device:TPU:9 now
where the time goes in v3:
time: 32.1 us; the launch traced here: 31.6 us
  Pallas kernels  29.7 us (93%)
  local copies, waits for them, and re-layouts  1.88 us (6%)
    pallas_call x1, Pallas kernels, body(): pl.pallas_call(kernel, out_shape=jax.ShapeDtypeStruct(gauge_links.shape,...  29.7 us
    unnamed x3, local copies, waits for them, and re-layouts  1.88 us

profile of v3, /device:TPU:9, one launch (start us, length us, event | category | flops | bytes accessed | tf_op | source)
XLA Modules:
  0.0 31.6 jit_solution(12775122608960936717)
XLA Ops:
  0.0 0.0 copy-start
  0.0 1.1 %copy-done = f32[4,2,3,3,2,4,256]{6,5,4,3,2,1,0:T(4,128)S(1)} copy-done((f32[4,2,3,3,2,4,256]{6,5,4,3,2,1,0:T(4,128)S(1)}, f32[4,2,3,3,2,4,256]{6,5,4,3,2,1,0:T(4,128)}, u32[]{:S(2)}) %copy-start) | copy-done | bytes 589848
  1.1 29.7 %shard_map.17 = f32[4,2,3,3,2,4,256]{6,5,4,3,2,1,0:T(4,128)S(1)} custom-call(f32[4,2,3,3,2,4,256]{6,5,4,3,2,1,0:T(4,128)S(1)} %copy-done), custom_call_target="tpu_custom_call" | custom-call | tf_op jit(solution)/shard_map/pallas_call | solution.py:671
  30.8 0.8 %copy.3 = f32[4,2,3,3,2,4,256]{6,5,4,3,2,1,0:T(4,128)} copy(f32[4,2,3,3,2,4,256]{6,5,4,3,2,1,0:T(4,128)S(1)} %shard_map.17) | data formatting | bytes 1179648
Async XLA Ops:
  0.0 1.1 %copy-start = (f32[4,2,3,3,2,4,256]{6,5,4,3,2,1,0:T(4,128)S(1)}, f32[4,2,3,3,2,4,256]{6,5,4,3,2,1,0:T(4,128)}, u32[]{:S(2)}) copy-start(f32[4,2,3,3,2,4,256]{6,5,4,3,2,1,0:T(4,128)} %x_ref.1) | copy-start | bytes 1769476

commit v4 on v3

--- a/solution.py
+++ b/solution.py
@@ -86,7 +86,7 @@
 
 
 def kernel(
-    x_ref, o_ref, U, XH, CH, PK0, PK3, RL, acc, Q, SQ, CQ, EH, XQ, OUT, hs, hr, cs, cr, io
+    x_ref, o_ref, U, XH, CH, PK0, PK3, RL, acc, KT, Q, SQ, CQ, EH, XQ, OUT, hs, hr, cs, cr, io
 ):
     ta = lax.axis_index("ta")
     gx = lax.axis_index("gx")
@@ -261,7 +261,28 @@
         p2 = mm(um, yz_shift(ut, m, 1))
         add(m, 0, mm(ut, p2, da=True))
 
-    def plane_tx(w):
+    def keep(slot, pair):
+        KT[slot, 0] = pair[0]
+        KT[slot, 1] = pair[1]
+
+    def tx_local(w):
+        for s in (1, 2):
+            ut, ux, uxt = ld(U, w, s, 0), ld(U, w, s, 1), ld(U, w, s + 1, 1)
+            p1 = mm(ut, uxt)
+            keep(s - 1, p1)
+            keep(s + 1, mm(ux, p1, da=True))
+
+    def tx_upper(w):
+        for s in (1, 2):
+            ux, uxt = ld(U, w, s, 1), ld(U, w, s + 1, 1)
+            utx = x_next(ld(U, w, s, 0), XH[w, 0], s - 1)
+            p2 = mm(ux, utx)
+            keep(s + 3, utx)
+            add(0, s - 1, mm(p2, uxt, db=True))
+            if s == 1:
+                keep(6, p2)
+
+    def tx_lower(w):
         cx_re, cx_im = unpacked(CH[w, 1])
         far_re, far_im = unpacked(CH[w, 4])
         cx = (cx_re, cx_im)
@@ -270,21 +291,18 @@
         )
         ct = unpacked(CH[w, 0])
         lower_c = mm(cx, mm(ct, cxt), da=True)
-        for s in (0, 1, 2):
-            ut, ux = ld(U, w, s, 0), ld(U, w, s, 1)
-            if s == 0:
-                utx = x_next(ut, XH[w, 1], 1)
-            else:
-                utx = x_next(ut, XH[w, 0], s - 1)
-            p2 = mm(ux, utx)
-            if s < 2:
-                add(1, s, mm(ut, p2, da=True))
-            if s > 0:
-                uxt = ld(U, w, s + 1, 1)
-                p1 = mm(ut, uxt)
-                add(0, s - 1, mm(p2, uxt, db=True))
-                add(1, s - 1, mm(p1, utx, db=True))
-                add(0, s - 1, x_prev(mm(ux, p1, da=True), lower_c, s - 1))
+        for s in range(2):
+            add(0, s, x_prev(ld(KT, 2 + s), lower_c, s))
+
+    def tx_side(w):
+        for s in range(2):
+            add(1, s, mm(ld(KT, s), ld(KT, 4 + s), db=True))
+        add(1, 1, mm(ld(U, w, 1, 0), ld(KT, 6), da=True))
+
+    def tx_before(w):
+        ut = ld(U, w, 0, 0)
+        p2 = mm(ld(U, w, 0, 1), x_next(ut, XH[w, 1], 1))
+        add(1, 0, mm(ut, p2, da=True))
 
     def plane_x(w, m):
         cx, cm = unpacked(CH[w, 1]), unpacked(CH[w, m])
@@ -482,11 +500,16 @@
         for c in range(2):
             Q[2, c] = q[c]
             Q[1, c] = jnp.where(lower, q[c], sroll(q[c], 4))
-        for k in (1, 3, 2):
+        for k in (2, 3, 1):
 
             @pl.when(chip + k < 4)
             def _():
                 half_to(k).start()
+
+        for k in (2, 3, 1):
+
+            @pl.when(chip + k < 4)
+            def _():
                 for h in range(2):
                     column_to(k, h).start()
 
@@ -523,6 +546,7 @@
         if m != 0:
             third_face(3, m)
     sweep_time(0)
+    tx_local(0)
     wait_x(0)
     for m in range(4):
         third_cols(CH, m)
@@ -530,39 +554,52 @@
             third_cols(XH, m)
     for m in (2, 3):
         plane_x(0, m)
-    then_left().wait_recv()
-    then_right().wait_recv()
-    third_cols(XH, 1)
-    third_cols(CH, 4)
-    plane_tx(0)
-    for m in range(4):
+
+    def finish(m):
         unitarise(0, m)
         pack(1, m)
-        if m == 0:
-            corner_up(1).start()
         if m == 1:
             corner_down(1).start()
         right(1, m).start()
         if m != 1:
             left(1, m).start()
+        if m == 0:
+            corner_up(1).start()
         up(1, m).start()
         if m != 0:
             down(1, m).start()
 
+    finish(2)
+    finish(3)
+    tx_upper(0)
+    tx_side(0)
+    then_left().wait_recv()
+    third_cols(XH, 1)
+    tx_before(0)
+    finish(1)
+    then_right().wait_recv()
+    third_cols(CH, 4)
+    tx_lower(0)
+    finish(0)
+
     sweep_start(1)
     wait_time(1)
     sweep_time(1)
+    tx_local(1)
     wait_x(1)
-    corner_up(1).wait_recv()
+    tx_upper(1)
     corner_down(1).wait_recv()
-    plane_tx(1)
+    tx_lower(1)
     unitarise(1, 0)
     chain_start()
     pack(2, 0)
     left(2, 0).start()
+    tx_side(1)
     for m in (2, 3):
         plane_x(1, m)
     chain_middle()
+    corner_up(1).wait_recv()
+    tx_before(1)
     for m in (1, 2, 3):
         unitarise(1, m)
 
@@ -681,6 +718,7 @@
             pltpu.VMEM((3, 4) + field[1:], f32),
             pltpu.VMEM((2, 2) + field[2:], f32),
             pltpu.VMEM((4, 2) + field, f32),
+            pltpu.VMEM((7,) + field, f32),
             pltpu.VMEM((4,) + field, f32),
             pltpu.VMEM(field, f32),
             pltpu.VMEM((3,) + field, f32),
@@ -696,7 +734,7 @@
         compiler_params=pltpu.CompilerParams(
             collective_id=0, has_side_effects=True, vmem_limit_bytes=32 * 2**20
         ),
-    )(gauge_links)
+    )(pltpu.with_memory_space_constraint(gauge_links, pltpu.HBM))
 
 
 def solution(mesh):

time: 32.1 us -> 29.8 us (0.928)
  local copies, waits for them, and re-layouts: 1.88 us -> 0.82 us
  Pallas kernels: 29.7 us -> 28.8 us
    unnamed x3 -> x1, local copies, waits for them, and re-layouts: 1.88 us -> 0.82 us
    pallas_call x1, Pallas kernels: 29.7 us -> 28.8 us  [body(): pl.pallas_call(kernel, out_shape=jax.ShapeDtypeStruct(gauge_links.shape,...]
where the time goes in v4:
time: 29.8 us; the launch traced here: 29.6 us
  Pallas kernels  28.8 us (97%)
  local copies, waits for them, and re-layouts  0.82 us (3%)
    pallas_call x1, Pallas kernels, body(): pl.pallas_call(kernel, out_shape=jax.ShapeDtypeStruct(gauge_links.shape,...  28.8 us
    unnamed x1, local copies, waits for them, and re-layouts  0.82 us

profile of v4, /device:TPU:9, one launch (start us, length us, event | category | flops | bytes accessed | tf_op | source)
XLA Modules:
  0.0 29.6 jit_solution(8245417157392050427)
XLA Ops:
  0.0 28.8 %shard_map.17 = f32[4,2,3,3,2,4,256]{6,5,4,3,2,1,0:T(4,128)S(1)} custom-call(f32[4,2,3,3,2,4,256]{6,5,4,3,2,1,0:T(4,128)} %x_ref.1), custom_call_target="tpu_custom_call" | custom-call | tf_op jit(solution)/shard_map/pallas_call | solution.py:708
  28.8 0.8 %copy.3 = f32[4,2,3,3,2,4,256]{6,5,4,3,2,1,0:T(4,128)} copy(f32[4,2,3,3,2,4,256]{6,5,4,3,2,1,0:T(4,128)S(1)} %shard_map.17) | data formatting | bytes 1179648

commit v5 on v4

--- a/solution.py
+++ b/solution.py
@@ -180,6 +180,23 @@
     def corner_down(w):
         return copy(w, 17, cols(PK3, w, 1), cols(CH, w, 4), dev(-1, 1))
 
+    def up_all():
+        return copy(0, 4, U.at[0, 2, :, :, pl.ds(0, 2)], U.at[0, 0, :, :, pl.ds(0, 2)], dev(1, 0))
+
+    def down_all():
+        links = pl.ds(1, 3)
+        return copy(
+            0, 1, U.at[0, 1, links, :, pl.ds(0, 2)], U.at[0, 3, links, :, pl.ds(0, 2)], dev(-1, 0)
+        )
+
+    def left_yz():
+        links = pl.ds(2, 2)
+        return copy(0, 10, PK0.at[0, links, pl.ds(0, 2)], XH.at[0, links, pl.ds(0, 2)], dev(0, -1))
+
+    def right_xyz():
+        links = pl.ds(1, 3)
+        return copy(0, 13, PK3.at[0, links, pl.ds(0, 2)], CH.at[0, links, pl.ds(0, 2)], dev(0, 1))
+
     def first_up():
         return copy(0, 18, cols(PK0, 0, 0), RL.at[0], dev(1, 0))
 
@@ -227,14 +244,12 @@
     pl.semaphore_wait(barrier, 5)
     first_down().start()
     first_up().start()
-    for m in (1, 0, 2, 3):
-        right(0, m).start()
-        if m != 1:
-            left(0, m).start()
-    for m in range(4):
-        up(0, m).start()
-        if m != 0:
-            down(0, m).start()
+    right_xyz().start()
+    left_yz().start()
+    right(0, 0).start()
+    left(0, 0).start()
+    up_all().start()
+    down_all().start()
 
     def plane_yz(w):
         for s in (1, 2):
@@ -529,31 +544,31 @@
             if m != 0:
                 down(w, m).wait_recv()
 
-    def wait_x(w):
-        for m in range(4):
-            right(w, m).wait_recv()
-            if m != 1:
-                left(w, m).wait_recv()
-
     sweep_start(0)
     first_down().wait_recv()
     then_right().start()
     first_up().wait_recv()
     then_left().start()
-    wait_time(0)
+    up_all().wait_recv()
+    down_all().wait_recv()
     for m in range(4):
         third_face(0, m)
         if m != 0:
             third_face(3, m)
     sweep_time(0)
     tx_local(0)
-    wait_x(0)
-    for m in range(4):
+    right_xyz().wait_recv()
+    left_yz().wait_recv()
+    third_cols(CH, 1)
+    for m in (2, 3):
         third_cols(CH, m)
+        third_cols(XH, m)
+        plane_x(0, m)
+
+    def arrived(m):
+        right(1, m).wait_recv()
         if m != 1:
-            third_cols(XH, m)
-    for m in (2, 3):
-        plane_x(0, m)
+            left(1, m).wait_recv()
 
     def finish(m):
         unitarise(0, m)
@@ -571,22 +586,27 @@
 
     finish(2)
     finish(3)
+    right(0, 0).wait_recv()
+    left(0, 0).wait_recv()
+    third_cols(CH, 0)
+    third_cols(XH, 0)
     tx_upper(0)
     tx_side(0)
+    then_right().wait_recv()
+    third_cols(CH, 4)
+    tx_lower(0)
+    finish(0)
     then_left().wait_recv()
     third_cols(XH, 1)
     tx_before(0)
     finish(1)
-    then_right().wait_recv()
-    third_cols(CH, 4)
-    tx_lower(0)
-    finish(0)
 
     sweep_start(1)
     wait_time(1)
     sweep_time(1)
     tx_local(1)
-    wait_x(1)
+    arrived(0)
+    arrived(1)
     tx_upper(1)
     corner_down(1).wait_recv()
     tx_lower(1)
@@ -596,12 +616,28 @@
     left(2, 0).start()
     tx_side(1)
     for m in (2, 3):
+        arrived(m)
         plane_x(1, m)
     chain_middle()
     corner_up(1).wait_recv()
     tx_before(1)
     for m in (1, 2, 3):
         unitarise(1, m)
+
+    for c in (up_all, down_all, left_yz, right_xyz, first_up, first_down, then_left, then_right):
+        c().wait_send()
+    right(0, 0).wait_send()
+    left(0, 0).wait_send()
+    for m in range(4):
+        if m != 0:
+            down(1, m).wait_send()
+        up(1, m).wait_send()
+        if m != 1:
+            left(1, m).wait_send()
+        right(1, m).wait_send()
+    corner_up(1).wait_send()
+    corner_down(1).wait_send()
+    left(2, 0).wait_send()
 
     for k in (1, 2, 3):
 
@@ -640,17 +676,16 @@
         OUT[m, 0, :, :, s] = pair[0]
         OUT[m, 1, :, :, s] = pair[1]
 
-    def save(m, t, h):
+    def save(m, h):
         return pltpu.make_async_copy(
-            OUT.at[m, :, :, :, t, pl.ds(4 * h, 4), :],
-            o_ref.at[m, :, :, :, t, :, pl.ds(h * LANES, LANES)],
-            io.at[4 * m + 2 * t + h],
+            OUT.at[m, :, :, :, :, pl.ds(4 * h, 4), :],
+            o_ref.at[m, :, :, :, :, :, pl.ds(h * LANES, LANES)],
+            io.at[4 + 2 * m + h],
         )
 
     def save_all(m):
-        for t in range(2):
-            for h in range(2):
-                save(m, t, h).start()
+        for h in range(2):
+            save(m, h).start()
 
     store(0, 0, mm(g2, g2, db=True))
     store(0, 1, mm(g3, g3, db=True))
@@ -664,22 +699,6 @@
         store(1, s, mm(mm(gs[s], ld(U, 2, 1 + s, 1)), gx_next, db=True))
     save_all(1)
 
-    for w in range(2):
-        for m in range(4):
-            if m != 0:
-                down(w, m).wait_send()
-            up(w, m).wait_send()
-            if m != 1:
-                left(w, m).wait_send()
-            right(w, m).wait_send()
-        if w == 1:
-            corner_up(w).wait_send()
-            corner_down(w).wait_send()
-    first_up().wait_send()
-    first_down().wait_send()
-    then_left().wait_send()
-    then_right().wait_send()
-    left(2, 0).wait_send()
     to_sibling().wait_send()
     entering_to_sibling().wait_send()
 
@@ -697,9 +716,8 @@
                 column_to(k, h).wait_send()
 
     for m in range(4):
-        for t in range(2):
-            for h in range(2):
-                save(m, t, h).wait()
+        for h in range(2):
+            save(m, h).wait()
 
 
 def body(gauge_links):

time: 29.8 us -> 29.6 us (level)
  no operation moved by 1% of the time
where the time goes in v5:
time: 29.6 us; the launch traced here: 29.5 us
  Pallas kernels  28.6 us (97%)
  local copies, waits for them, and re-layouts  0.82 us (3%)
    pallas_call x1, Pallas kernels, body(): pl.pallas_call(kernel, out_shape=jax.ShapeDtypeStruct(gauge_links.shape,...  28.6 us
    unnamed x1, local copies, waits for them, and re-layouts  0.82 us

profile of v5, /device:TPU:9, one launch (start us, length us, event | category | flops | bytes accessed | tf_op | source)
XLA Modules:
  0.0 29.5 jit_solution(9286672038300115647)
XLA Ops:
  0.0 28.6 %shard_map.17 = f32[4,2,3,3,2,4,256]{6,5,4,3,2,1,0:T(4,128)S(1)} custom-call(f32[4,2,3,3,2,4,256]{6,5,4,3,2,1,0:T(4,128)} %x_ref.1), custom_call_target="tpu_custom_call" | custom-call | tf_op jit(solution)/shard_map/pallas_call | solution.py:726
  28.6 0.8 %copy.3 = f32[4,2,3,3,2,4,256]{6,5,4,3,2,1,0:T(4,128)} copy(f32[4,2,3,3,2,4,256]{6,5,4,3,2,1,0:T(4,128)S(1)} %shard_map.17) | data formatting | bytes 1179648

commit v6 on v5

--- a/solution.py
+++ b/solution.py
@@ -261,10 +261,25 @@
             add(2, s - 1, yz_shift(mm(uz, p1, da=True), 3, -1))
             add(3, s - 1, yz_shift(mm(uy, p2, da=True), 2, -1))
 
+    def keep(slot, pair):
+        KT[slot, 0] = pair[0]
+        KT[slot, 1] = pair[1]
+
+    def local_t(w, m):
+        keep(5 + m, mm(ld(U, w, 2, m), yz_shift(ld(U, w, 2, 0), m, 1)))
+
+    def local_x(w, m):
+        for s in (1, 2):
+            ux, um = ld(U, w, s, 1), ld(U, w, s, m)
+            p2 = mm(um, yz_shift(ux, m, 1))
+            keep(5 + 2 * m + s, p2)
+            keep(9 + 2 * m + s, mm(ux, p2, da=True))
+
     def plane_t(w, m, s):
         ut, um, umt = ld(U, w, s, 0), ld(U, w, s, m), ld(U, w, s + 1, m)
         utm = yz_shift(ut, m, 1)
-        p1, p2 = mm(ut, umt), mm(um, utm)
+        p1 = mm(ut, umt)
+        p2 = mm(um, utm) if s == 1 else ld(KT, 5 + m)
         add(0, s - 1, mm(p2, umt, db=True))
         add(m, s - 1, mm(p1, utm, db=True))
         add(0, s - 1, yz_shift(mm(um, p1, da=True), m, -1))
@@ -276,16 +291,11 @@
         p2 = mm(um, yz_shift(ut, m, 1))
         add(m, 0, mm(ut, p2, da=True))
 
-    def keep(slot, pair):
-        KT[slot, 0] = pair[0]
-        KT[slot, 1] = pair[1]
-
-    def tx_local(w):
-        for s in (1, 2):
-            ut, ux, uxt = ld(U, w, s, 0), ld(U, w, s, 1), ld(U, w, s + 1, 1)
-            p1 = mm(ut, uxt)
-            keep(s - 1, p1)
-            keep(s + 1, mm(ux, p1, da=True))
+    def tx_local(w, s):
+        ut, ux, uxt = ld(U, w, s, 0), ld(U, w, s, 1), ld(U, w, s + 1, 1)
+        p1 = mm(ut, uxt)
+        keep(s - 1, p1)
+        keep(s + 1, mm(ux, p1, da=True))
 
     def tx_upper(w):
         for s in (1, 2):
@@ -326,11 +336,11 @@
             ux, um = ld(U, w, s, 1), ld(U, w, s, m)
             umx = x_next(um, XH[w, m], s - 1)
             uxm = yz_shift(ux, m, 1)
-            p1, p2 = mm(ux, umx), mm(um, uxm)
+            p1, p2 = mm(ux, umx), ld(KT, 5 + 2 * m + s)
             add(1, s - 1, mm(p2, umx, db=True))
             add(m, s - 1, mm(p1, uxm, db=True))
             add(1, s - 1, yz_shift(mm(um, p1, da=True), m, -1))
-            add(m, s - 1, x_prev(mm(ux, p2, da=True), lower_c, s - 1))
+            add(m, s - 1, x_prev(ld(KT, 9 + 2 * m + s), lower_c, s - 1))
 
     def unitarise(w, m):
         scale = ape_weight / 6.0
@@ -532,6 +542,10 @@
         plane_yz(w)
         for m in (2, 3):
             plane_t(w, m, 1)
+            local_t(w, m)
+        tx_local(w, 1)
+        for m in (2, 3):
+            local_x(w, m)
 
     def sweep_time(w):
         for m in (2, 3):
@@ -556,7 +570,7 @@
         if m != 0:
             third_face(3, m)
     sweep_time(0)
-    tx_local(0)
+    tx_local(0, 2)
     right_xyz().wait_recv()
     left_yz().wait_recv()
     third_cols(CH, 1)
@@ -604,7 +618,7 @@
     sweep_start(1)
     wait_time(1)
     sweep_time(1)
-    tx_local(1)
+    tx_local(1, 2)
     arrived(0)
     arrived(1)
     tx_upper(1)
@@ -736,7 +750,7 @@
             pltpu.VMEM((3, 4) + field[1:], f32),
             pltpu.VMEM((2, 2) + field[2:], f32),
             pltpu.VMEM((4, 2) + field, f32),
-            pltpu.VMEM((7,) + field, f32),
+            pltpu.VMEM((18,) + field, f32),
             pltpu.VMEM((4,) + field, f32),
             pltpu.VMEM(field, f32),
             pltpu.VMEM((3,) + field, f32),

time: 29.6 us -> 29.3 us (0.990)
  Pallas kernels: 28.6 us -> 28.3 us
    pallas_call x1, Pallas kernels: 28.6 us -> 28.3 us  [body(): pl.pallas_call(kernel, out_shape=jax.ShapeDtypeStruct(gauge_links.shape,...]
where the time goes in v6:
time: 29.3 us; the launch traced here: 29.1 us
  Pallas kernels  28.3 us (97%)
  local copies, waits for them, and re-layouts  0.82 us (3%)
    pallas_call x1, Pallas kernels, body(): pl.pallas_call(kernel, out_shape=jax.ShapeDtypeStruct(gauge_links.shape,...  28.3 us
    unnamed x1, local copies, waits for them, and re-layouts  0.82 us

profile of v6, /device:TPU:9, one launch (start us, length us, event | category | flops | bytes accessed | tf_op | source)
XLA Modules:
  0.0 29.1 jit_solution(16364588170363901130)
XLA Ops:
  0.0 28.3 %shard_map.17 = f32[4,2,3,3,2,4,256]{6,5,4,3,2,1,0:T(4,128)S(1)} custom-call(f32[4,2,3,3,2,4,256]{6,5,4,3,2,1,0:T(4,128)} %x_ref.1), custom_call_target="tpu_custom_call" | custom-call | tf_op jit(solution)/shard_map/pallas_call | solution.py:740
  28.3 0.8 %copy.3 = f32[4,2,3,3,2,4,256]{6,5,4,3,2,1,0:T(4,128)} copy(f32[4,2,3,3,2,4,256]{6,5,4,3,2,1,0:T(4,128)S(1)} %shard_map.17) | data formatting | bytes 1179648

commit v7 on v6

--- a/solution.py
+++ b/solution.py
@@ -563,6 +563,14 @@
     then_right().start()
     first_up().wait_recv()
     then_left().start()
+    right_xyz().wait_recv()
+    left_yz().wait_recv()
+    third_cols(CH, 1)
+    for m in (2, 3):
+        third_cols(CH, m)
+        third_cols(XH, m)
+        plane_x(0, m)
+
     up_all().wait_recv()
     down_all().wait_recv()
     for m in range(4):
@@ -571,14 +579,6 @@
             third_face(3, m)
     sweep_time(0)
     tx_local(0, 2)
-    right_xyz().wait_recv()
-    left_yz().wait_recv()
-    third_cols(CH, 1)
-    for m in (2, 3):
-        third_cols(CH, m)
-        third_cols(XH, m)
-        plane_x(0, m)
-
     def arrived(m):
         right(1, m).wait_recv()
         if m != 1:

time: 29.3 us -> 29.1 us (level)
  no operation moved by 1% of the time
where the time goes in v7:
time: 29.1 us; the launch traced here: 29 us
  Pallas kernels  28.1 us (97%)
  local copies, waits for them, and re-layouts  0.82 us (3%)
    pallas_call x1, Pallas kernels, body(): pl.pallas_call(kernel, out_shape=jax.ShapeDtypeStruct(gauge_links.shape,...  28.1 us
    unnamed x1, local copies, waits for them, and re-layouts  0.82 us

profile of v7, /device:TPU:9, one launch (start us, length us, event | category | flops | bytes accessed | tf_op | source)
XLA Modules:
  0.0 29.0 jit_solution(13170730187113433457)
XLA Ops:
  0.0 28.1 %shard_map.17 = f32[4,2,3,3,2,4,256]{6,5,4,3,2,1,0:T(4,128)S(1)} custom-call(f32[4,2,3,3,2,4,256]{6,5,4,3,2,1,0:T(4,128)} %x_ref.1), custom_call_target="tpu_custom_call" | custom-call | tf_op jit(solution)/shard_map/pallas_call | solution.py:740
  28.2 0.8 %copy.3 = f32[4,2,3,3,2,4,256]{6,5,4,3,2,1,0:T(4,128)} copy(f32[4,2,3,3,2,4,256]{6,5,4,3,2,1,0:T(4,128)S(1)} %shard_map.17) | data formatting | bytes 1179648

commit v8 on v7

--- a/solution.py
+++ b/solution.py
@@ -246,10 +246,10 @@
     first_up().start()
     right_xyz().start()
     left_yz().start()
+    up_all().start()
+    down_all().start()
     right(0, 0).start()
     left(0, 0).start()
-    up_all().start()
-    down_all().start()
 
     def plane_yz(w):
         for s in (1, 2):

time: 29.1 us -> 29.1 us (level)
  no operation moved by 1% of the time
where the time goes in v8:
time: 29.1 us; the launch traced here: 29 us
  Pallas kernels  28.1 us (97%)
  local copies, waits for them, and re-layouts  0.82 us (3%)
    pallas_call x1, Pallas kernels, body(): pl.pallas_call(kernel, out_shape=jax.ShapeDtypeStruct(gauge_links.shape,...  28.1 us
    unnamed x1, local copies, waits for them, and re-layouts  0.82 us

profile of v8, /device:TPU:9, one launch (start us, length us, event | category | flops | bytes accessed | tf_op | source)
XLA Modules:
  0.0 29.0 jit_solution(13484849876818232497)
XLA Ops:
  0.0 28.1 %shard_map.17 = f32[4,2,3,3,2,4,256]{6,5,4,3,2,1,0:T(4,128)S(1)} custom-call(f32[4,2,3,3,2,4,256]{6,5,4,3,2,1,0:T(4,128)} %x_ref.1), custom_call_target="tpu_custom_call" | custom-call | tf_op jit(solution)/shard_map/pallas_call | solution.py:740
  28.2 0.8 %copy.3 = f32[4,2,3,3,2,4,256]{6,5,4,3,2,1,0:T(4,128)} copy(f32[4,2,3,3,2,4,256]{6,5,4,3,2,1,0:T(4,128)S(1)} %shard_map.17) | data formatting | bytes 1179648
